TPU v7x, 256 devices: a whole 4x4x8 slice. The times are simulated.
256 devices in a mesh: row: 64 (over z, x, core), col: 4 (over y).
Axes of the slice: x: 4, y: 4, z: 8, core: 2. Of those that a mesh axis runs over, the one named last changes fastest.
Arguments:
- panel: float32 [32768, 16384], P('row', 'col'), may hold values from -180 to 180, as said below
- sketch_matrix: float32 [16384, 512], P('col'), may hold values from -0.046875 to 0.046875
Outputs:
- projected: float32 [512, 16384], P('row', 'col')
- spread: float32 [512, 512], P('row')
Inputs may be any that keep to these rules, and one draw needn't show every extreme that they name: `panel`: activation rows with a spread of scales over rows and features.
All inputs are finite; a program needn't handle non-finite values.
Results may differ from a plain program's by a relative error of at most 0.00015.
Values sent between devices are 32-bit elements; how exact they have to be, the bound alone decides.
No kernel may reach another device: no remote copies, remote signals or barrier semaphores. Data moves between devices by JAX's collectives and lax.ppermute only.
A program may use at most 128 MiB of HBM per device.

v0:
```python
import math

import jax
import jax.numpy as jnp
from jax import lax
from jax.sharding import PartitionSpec as P


def inner_rows(left, right):
    return lax.dot_general(
        left,
        right,
        (((0,), (0,)), ((), ())),
        precision=lax.Precision.HIGHEST,
        preferred_element_type=jnp.float32,
    )


def shards(panel, sketch_matrix):
    highest = lax.Precision.HIGHEST
    sketch_width = sketch_matrix.shape[1]
    total_rows = panel.shape[0] * lax.axis_size("row")
    norm_scale = 1.0 / math.sqrt(total_rows)
    partial_sketch = jnp.dot(
        panel, sketch_matrix, preferred_element_type=jnp.float32, precision=highest
    )
    own_rows = lax.psum(partial_sketch, "col")
    gram_sum = lax.psum(inner_rows(own_rows, own_rows), "row")
    lower_factor = jnp.linalg.cholesky(gram_sum)
    row_share = sketch_width // lax.axis_size("row")
    first_row = lax.axis_index("row") * row_share
    spread = lax.dynamic_slice_in_dim(lower_factor.T, first_row, row_share, 0) * norm_scale
    basis_part = jax.scipy.linalg.solve_triangular(lower_factor, own_rows.T, lower=True)
    projected = (
        lax.psum_scatter(
            jnp.dot(basis_part, panel, preferred_element_type=jnp.float32, precision=highest),
            "row",
            scatter_dimension=0,
            tiled=True,
        )
        * norm_scale
    )
    return (projected, spread)


def solution(mesh):
    return jax.shard_map(
        shards,
        mesh=mesh,
        in_specs=(P("row", "col"), P("col", None)),
        out_specs=(P("row", "col"), P("row", None)),
        check_vma=False,
    )
```

profile of v0, /device:TPU:1, one launch (start us, length us, event | category | flops | bytes accessed | tf_op | source)
XLA Modules:
  0.0 643.8 jit_solution(13430664622619193812)
XLA Ops:
  7.2 17.3 %fusion.41 = f32[512,512]{1,0:T(8,128)} fusion(f32[512,4096]{1,0:T(8,128)} %param.2, f32[4096,512]{1,0:T(8,128)} %param.3), kind=kOutput, calls=%fused_computation.78 | convolution fusion | flops 12884901888 | bytes 17825792 | tf_op jit(solution)/shard_map/dot_general | solution.py:24
  24.6 53.5 %all-reduce.6.cloned.1.call-done = f32[512,512]{1,0:T(8,128)} async-done(((f32[512,512]{1,0:T(8,128)}), f32[512,512]{1,0:T(8,128)}) %all-reduce.6.cloned.1.call-update) | async-done | bytes 1048592 | tf_op jit(solution)/shard_map/psum | solution.py:27
  78.1 4.4 fusion.42
  83.0 185.5 %all-reduce.8.cloned.1.call-done = f32[512,512]{0,1:T(8,128)} async-done(((f32[512,512]{0,1:T(8,128)}), f32[512,512]{0,1:T(8,128)}) %all-reduce.8.cloned.1.call-update) | async-done | bytes 1048592 | tf_op jit(solution)/shard_map/psum | solution.py:28
  268.5 1.6 copy.11
  270.1 1.4 fusion.8
  271.6 11.7 %cholesky.104 = f32[128,128]{1,0:T(8,128)S(1)} custom-call(f32[128,128]{1,0:T(8,128)S(1)} %cholesky.266), custom_call_target="Cholesky" | custom-call | tf_op jit(solution)/shard_map/jit(cholesky)/cholesky | solution.py:29
  283.9 9.8 %custom-call.31 = f32[1,128,128]{1,2,0:T(8,128)S(1)} custom-call(f32[1,128,128]{2,1,0:T(8,128)S(1)} %get-tuple-element.35), custom_call_target="InvertDiagBlocksLowerTriangular" | custom-call | tf_op jit(solution)/shard_map/jit(cholesky)/cholesky | solution.py:29
  294.8 12.3 %cholesky.217 = f32[128,128]{1,0:T(8,128)} custom-call(f32[128,128]{1,0:T(8,128)S(1)} %cholesky.270), custom_call_target="Cholesky" | custom-call | tf_op jit(solution)/shard_map/jit(cholesky)/cholesky | solution.py:29
  309.0 10.0 %custom-call.32 = f32[1,128,128]{1,2,0:T(8,128)S(1)} custom-call(f32[1,128,128]{2,1,0:T(8,128)S(1)} %get-tuple-element.32), custom_call_target="InvertDiagBlocksLowerTriangular" | custom-call | tf_op jit(solution)/shard_map/jit(cholesky)/cholesky | solution.py:29
  319.6 11.7 %cholesky.238 = f32[128,128]{1,0:T(8,128)S(1)} custom-call(f32[128,128]{1,0:T(8,128)S(1)} %cholesky.275), custom_call_target="Cholesky" | custom-call | tf_op jit(solution)/shard_map/jit(cholesky)/cholesky | solution.py:29
  332.1 9.8 %custom-call.33 = f32[1,128,128]{1,2,0:T(8,128)S(1)} custom-call(f32[1,128,128]{2,1,0:T(8,128)S(1)} %get-tuple-element.29), custom_call_target="InvertDiagBlocksLowerTriangular" | custom-call | tf_op jit(solution)/shard_map/jit(cholesky)/cholesky | solution.py:29
  342.5 11.9 %cholesky.255 = f32[128,128]{1,0:T(8,128)S(1)} custom-call(f32[128,128]{1,0:T(8,128)S(1)} %convolution_subtract_fusion.5), custom_call_target="Cholesky" | custom-call | tf_op jit(solution)/shard_map/jit(cholesky)/cholesky | solution.py:29
  358.3 1.3 fusion.9
  359.5 10.9 %while.1 = (s32[]{:T(128)}, f32[512,512]{1,0:T(8,128)S(1)}, s32[4,2]{0,1:T(2,128)S(1)}, f32[4,128,128]{2,1,0:T(8,128)}, s32[]{:T(128)}) while((s32[]{:T(128)}, f32[512,512]{1,0:T(8,128)S(1)}, s32[4,2]{0,1:T(2,128)S(1)}, f32[4,128,128]{2,1,0:T(8,128)}, s32[]{:T(128)}) %tuple.33), condition=%wide.while_cond, body=%wide.while_body.sunk | while | flops 2 | bytes 132205 | solution.py:33
  360.2 2.1 bitcast_dynamic-update-slice_fusion.2
  362.9 2.1 bitcast_dynamic-update-slice_fusion.2
  365.6 2.1 bitcast_dynamic-update-slice_fusion.2
  368.3 2.0 bitcast_dynamic-update-slice_fusion.2
  370.4 40.1 %custom-call.34 = f32[4,128,128]{1,2,0:T(8,128)S(1)} custom-call(f32[4,128,128]{2,1,0:T(8,128)} %get-tuple-element.9), custom_call_target="InvertDiagBlocksLowerTriangular" | custom-call | tf_op jit(solution)/shard_map/jit(_solve_triangular)/triangular_solve | solution.py:33
  413.4 1.5 convolution_subtract_fusion.2
  415.3 17.2 %fusion = f32[512,4096]{1,0:T(8,128)} fusion(f32[512,4096]{1,0:T(8,128)} %param.2, f32[128,512]{1,0:T(8,128)S(1)} %fusion.28, f32[128,512]{1,0:T(8,128)S(1)} %fusion.29, f32[128,512]{1,0:T(8,128)S(1)} %fusion.31, f32[128,512]{1,0:T(8,128)S(1)} %fusion.18), kind=kOutput, calls=%fused_computation.10 | convolution fusion | flops 12885688320 | bytes 17825792 | tf_op jit(solution)/shard_map/dot_general | solution.py:36
  436.3 199.2 %all-reduce.10.cloned.1.call-done = f32[512,4096]{1,0:T(8,128)} async-done(((f32[512,4096]{1,0:T(8,128)}), f32[512,4096]{1,0:T(8,128)}) %all-reduce.10.cloned.1.call-update) | async-done | bytes 8388624
  635.5 1.6 dynamic-slice_multiply_fusion
  (51 shorter events, 16.5 us)
Async XLA Ops:
  7.2 70.9 %all-reduce.6.cloned.1.call-start = ((), (), s32[]{:S(2)}) async-start(), calls=%async_computation | async-start | bytes 2097152 | tf_op jit(solution)/shard_map/psum | solution.py:27
  24.6 244.0 %all-reduce.8.cloned.1.call-start = ((), (), s32[]{:S(2)}) async-start(), calls=%async_computation.1 | async-start | bytes 2097152 | tf_op jit(solution)/shard_map/psum | solution.py:28
  82.5 328.0 %copy-start = (f32[512,512]{1,0:T(8,128)S(1)}, f32[512,512]{1,0:T(8,128)}, u32[]{:S(2)}) copy-start(f32[512,512]{1,0:T(8,128)} %all-reduce.6.cloned.1.call-done) | copy-start | bytes 3145732
  82.5 552.9 %all-reduce.10.cloned.1.call-start = ((), (), s32[]{:S(2)}) async-start(), calls=%async_computation.2 | async-start | bytes 16777216
  283.3 0.6 copy-start.1
  432.6 0.7 copy-start.2
Sparse Core Ops, SparseCore 0:
  24.7 53.3 all-reduce.5
  82.6 185.8 all-reduce.7
  432.7 202.6 all-reduce.9
where the time goes:
time: 649 us; the launch traced here: 644 us
  waiting for transfers between devices  438 us (67%)
  other arithmetic  126 us (19%)
  matrix products  45.9 us (7%)
  between operations  17.4 us (3%)
  local copies, waits for them, and re-layouts  16.1 us (2%)
    unnamed x4, waiting for transfers between devices  199 us
    psum x1, waiting for transfers between devices, shards(): gram_sum = lax.psum(inner_rows(own_rows, own_rows), 'row')  185 us
    another operation x14, other arithmetic, shards(): lower_factor = jnp.linalg.cholesky(gram_sum)  80.2 us
    psum x1, waiting for transfers between devices, shards(): own_rows = lax.psum(partial_sketch, 'col')  53.5 us
    another operation x3, other arithmetic, shards(): jax.scipy.linalg.solve_triangular(lower_factor, own_rows.T, lower=True)  41.4 us
    dot_general x1, matrix products, shards(): jnp.dot(panel, sketch_matrix, preferred_element_type=jnp.float32, precisi...  17.3 us
    dot_general x1, matrix products, shards(): jnp.dot(basis_part, panel, preferred_element_type=jnp.float32, precision=...  17.2 us
  transfers between devices with their start and end apart: 3, of which 3 were waited for; matrix products, arithmetic and copies ran while one was open for 0% of the time, Pallas kernels for 0%

commit v1 on v0

v1 whole, which is shorter than its diff:
```python
import functools
import math

import jax
import jax.numpy as jnp
from jax import lax
from jax.experimental import pallas as pl
from jax.experimental.pallas import tpu as pltpu
from jax.sharding import PartitionSpec as P

ZS, XS, CS, YS = 8, 4, 2, 4
BLOCK = 128
PIVOTS = 32
WIDTH = 512
F32, BF16 = jnp.float32, jnp.bfloat16


def row_index(z, x, c):
    return ((z % ZS) * XS + x % XS) * CS + c


def row_pairs(move):
    return [
        (row_index(z, x, c), row_index(*move(z, x, c)))
        for z in range(ZS)
        for x in range(XS)
        for c in range(CS)
    ]


Z_GROUPS = [[row_index(z, x, c) for z in range(ZS)] for x in range(XS) for c in range(CS)]
ZX_GROUPS = [[row_index(z, x, c) for z in range(ZS) for x in range(XS)] for c in range(CS)]


def send_y(array, step):
    return lax.ppermute(array, "col", [(i, (i + step) % YS) for i in range(YS)])


def swap_core(array):
    return lax.ppermute(array, "row", row_pairs(lambda z, x, c: (z, x, 1 - c)))


def exchange(array, groups):
    return lax.all_to_all(array, "row", 0, 0, axis_index_groups=groups)


def repeat(array, times):
    return jnp.broadcast_to(array[None], (times,) + array.shape)


def together(*arrays):
    return lax.optimization_barrier(arrays)


def ring_sum_y(ahead, behind, next_head, before_tail, own):
    half = own.shape[0] // 2
    from_before, from_after = together(send_y(ahead, 1), send_y(behind, -1))
    head, tail = together(next_head + from_before[:half], before_tail + from_after[half:])
    head, tail = together(send_y(head, 1), send_y(tail, -1))
    return own + jnp.concatenate([from_after[:half] + head, from_before[half:] + tail], 0)


def ring_gather_y(own):
    half = own.shape[0] // 2
    before, after = together(send_y(own, 1), send_y(own, -1))
    return own, before, after, send_y(before[:half], 1), send_y(after[half:], -1)


def place(blocks, size, position):
    own = blocks[0]
    out = jnp.zeros((size,) + own.shape, own.dtype)
    for k, block in blocks.items():
        out = lax.dynamic_update_index_in_dim(out, block, (position + k) % size, 0)
    return out


def split(array):
    high = array.astype(BF16)
    return high, (array - high.astype(F32)).astype(BF16)


def dot(left, right):
    return jnp.dot(left, right, preferred_element_type=F32)


def dot_parts(left, right):
    return dot(left[0], right[0]) + dot(left[0], right[1]) + dot(left[1], right[0])


def params(size):
    return pltpu.CompilerParams(vmem_limit_bytes=size * 2**20)


def cost(flops, size):
    return pl.CostEstimate(flops=flops, bytes_accessed=size, transcendentals=0)


IN_VMEM = pl.BlockSpec(memory_space=pltpu.VMEM)
IN_PLACE = pl.BlockSpec(memory_space=pl.ANY)
IN_SMEM = pl.BlockSpec(memory_space=pltpu.SMEM)


def sketch_kernel(
    y_ref, panel_ref, matrix_ref, ahead_ref, behind_ref, next_ref, before_ref, own_ref,
    panels, matrices, total, panel_sems, matrix_sems,
):
    steps, _, width = panels.shape

    def copies(k):
        at = pl.ds(pl.multiple_of(k * width, width), width)
        return (
            pltpu.make_async_copy(panel_ref.at[:, at], panels.at[k], panel_sems.at[k]),
            pltpu.make_async_copy(matrix_ref.at[at], matrices.at[k], matrix_sems.at[k]),
        )

    for k in range(steps):
        for copy in copies(k):
            copy.start()
    total[...] = jnp.zeros_like(total)

    def step(k, carry):
        for copy in copies(k):
            copy.wait()
        total[...] += dot_parts(split(panels[k]), split(matrices[k]))
        return carry

    lax.fori_loop(0, steps, step, 0)
    block = own_ref.shape[0]
    half = block // 2

    def rows(step, start, size):
        at = lax.rem(y_ref[0] + step, YS) * block + start
        return total[pl.ds(pl.multiple_of(at, half), size), :]

    ahead_ref[:half] = rows(2, 0, half)
    ahead_ref[half:] = rows(1, half, half)
    behind_ref[:half] = rows(3, 0, half)
    behind_ref[half:] = rows(2, half, half)
    next_ref[...] = rows(1, 0, half)
    before_ref[...] = rows(3, half, half)
    own_ref[...] = rows(0, 0, block)


def sketch_product(y, panel, matrix):
    rows, depth = panel.shape
    rank = matrix.shape[1]
    steps = depth // WIDTH
    block = rows // YS
    whole = jax.ShapeDtypeStruct((block, rank), F32)
    half = jax.ShapeDtypeStruct((block // 2, rank), F32)
    return pl.pallas_call(
        sketch_kernel,
        in_specs=[IN_SMEM, IN_PLACE, IN_PLACE],
        out_specs=(IN_VMEM,) * 5,
        out_shape=(whole, whole, half, half, whole),
        scratch_shapes=[
            pltpu.VMEM((steps, rows, WIDTH), F32),
            pltpu.VMEM((steps, WIDTH, rank), F32),
            pltpu.VMEM((rows, rank), F32),
            pltpu.SemaphoreType.DMA((steps,)),
            pltpu.SemaphoreType.DMA((steps,)),
        ],
        compiler_params=params(54),
        cost_estimate=cost(6 * rows * rank * depth, 4 * depth * (rows + rank)),
        name="sketch_product",
    )(y, panel, matrix)


def place_kernel(y_ref, own, before, after, head, tail, out_ref):
    y = y_ref[0]
    at = lambda step: lax.rem(y + step, YS)
    half = out_ref.shape[1] // 2
    out_ref[at(0)] = own[...]
    out_ref[at(3)] = before[...]
    out_ref[at(1)] = after[...]
    out_ref[at(2), :half] = head[...]
    out_ref[at(2), half:] = tail[...]


def place_blocks(y, blocks):
    rows, rank = blocks[0].shape
    return pl.pallas_call(
        place_kernel,
        in_specs=[IN_SMEM] + [IN_VMEM] * 5,
        out_specs=IN_VMEM,
        out_shape=jax.ShapeDtypeStruct((YS, rows, rank), F32),
        compiler_params=params(16),
        cost_estimate=cost(0, 8 * YS * rows * rank),
        name="place_blocks",
    )(y, *blocks).reshape(YS * rows, rank)


def gram_kernel(
    y_ref, core_ref, own_ref, other_ref, gram_ref, own_high, own_low, other_high, other_low,
    parts, turned, sems,
):
    outs = (own_high, own_low, other_high, other_low)
    leave = lambda k: pltpu.make_async_copy(parts.at[k], outs[k], sems.at[k])
    share = gram_ref.shape[0]
    total = None
    for k, sketch_ref in enumerate((own_ref, other_ref)):
        sketch = sketch_ref[...]
        high, low = split(sketch)
        parts[2 * k] = high
        parts[2 * k + 1] = low
        leave(2 * k).start()
        leave(2 * k + 1).start()
        block = CS * share
        columns = pl.ds(pl.multiple_of(y_ref[0] * block, block), block)
        turned[...] = sketch_ref[:, columns].T
        rows = turned[pl.ds(pl.multiple_of(core_ref[0] * share, share), share), :]
        term = dot_parts(split(rows), (high, low))
        total = term if total is None else total + term
    gram_ref[...] = total
    for k in range(4):
        leave(k).wait()


def gram_product(y, core, own, other):
    rows, rank = own.shape
    share = rank // (YS * CS)
    part = jax.ShapeDtypeStruct((rows, rank), BF16)
    return pl.pallas_call(
        gram_kernel,
        in_specs=[IN_SMEM, IN_SMEM, IN_VMEM, IN_VMEM],
        out_specs=(IN_VMEM,) + (IN_PLACE,) * 4,
        out_shape=(jax.ShapeDtypeStruct((share, rank), F32),) + (part,) * 4,
        scratch_shapes=[
            pltpu.VMEM((4, rows, rank), BF16),
            pltpu.VMEM((CS * share, rows), F32),
            pltpu.SemaphoreType.DMA((4,)),
        ],
        compiler_params=params(24),
        cost_estimate=cost(12 * rows * rank * share, 16 * rows * rank),
        name="gram_product",
    )(y, core, own, other)


def project_kernel(
    core_ref, own_high, own_low, other_high, other_low, panel_ref, arrived_ref, out_ref,
    sketches, panels, arrived, outs, sketch_sems, panel_sems, arrived_sems, out_sems,
):
    steps, _, width = panels.shape
    base = core_ref[0] * (steps * width)

    def arrive(k):
        at = pl.ds(pl.multiple_of(base + k * width, width), width)
        return (
            pltpu.make_async_copy(panel_ref.at[:, at], panels.at[k], panel_sems.at[k]),
            pltpu.make_async_copy(arrived_ref.at[:, at], arrived.at[k], arrived_sems.at[k]),
        )

    def leave(k):
        at = pl.ds(pl.multiple_of(k * width, width), width)
        return pltpu.make_async_copy(outs.at[k], out_ref.at[at], out_sems.at[k])

    loads = [
        pltpu.make_async_copy(part, sketches.at[k], sketch_sems.at[k])
        for k, part in enumerate((own_high, own_low, other_high, other_low))
    ]
    for copy in loads:
        copy.start()
    for k in range(steps):
        for copy in arrive(k):
            copy.start()
    for copy in loads:
        copy.wait()

    def step(k, carry):
        for copy in arrive(k):
            copy.wait()
        own = dot_parts(split(panels[k].T), (sketches[0], sketches[1]))
        outs[k] = own + dot_parts(split(arrived[k].T), (sketches[2], sketches[3]))
        leave(k).start()
        return carry

    lax.fori_loop(0, steps, step, 0)
    for k in range(steps):
        leave(k).wait()


def project_product(core, sketches, panel, arrived):
    rows, rank = sketches[0].shape
    cols = panel.shape[1] // CS
    steps = cols // WIDTH
    return pl.pallas_call(
        project_kernel,
        in_specs=[IN_SMEM] + [IN_PLACE] * 6,
        out_specs=IN_PLACE,
        out_shape=jax.ShapeDtypeStruct((cols, rank), F32),
        scratch_shapes=[
            pltpu.VMEM((4, rows, rank), BF16),
            pltpu.VMEM((steps, rows, WIDTH), F32),
            pltpu.VMEM((steps, rows, WIDTH), F32),
            pltpu.VMEM((steps, WIDTH, rank), F32),
            pltpu.SemaphoreType.DMA((4,)),
            pltpu.SemaphoreType.DMA((steps,)),
            pltpu.SemaphoreType.DMA((steps,)),
            pltpu.SemaphoreType.DMA((steps,)),
        ],
        compiler_params=params(57),
        cost_estimate=cost(12 * rank * rows * cols, 12 * cols * (rows + rank)),
        name="project_product",
    )(core, *sketches, panel, arrived)


def exact_dot(left, right, dims):
    return lax.dot_general(
        left, right, (dims, ((), ())), precision=lax.Precision.HIGHEST, preferred_element_type=F32
    )


def eliminate(rows, base):
    tiles = len(rows)
    count = 8 * tiles
    lanes = BLOCK
    sub = lax.broadcasted_iota(jnp.int32, (8, lanes), 0)
    spread = lambda a, u: jnp.broadcast_to(a[u : u + 1, :], (8, lanes))
    columns = [
        [jnp.broadcast_to(row[:, base + t : base + t + 1], (8, lanes)) for row in rows]
        for t in range(count)
    ]
    parts = rows[0].shape[1] // lanes
    rows = [[row[:, lanes * q : lanes * (q + 1)] for q in range(parts)] for row in rows]
    scales = []
    for s in range(count):
        first, u = divmod(s, 8)
        pivot = spread(columns[s][first], u)
        scales.append(lax.rsqrt(pivot))
        inverse = 1.0 / pivot
        factor = {v: columns[s][v] * inverse for v in range(first, tiles)}
        factor[first] = jnp.where(sub > u, factor[first], 0.0)
        for t in range(s + 1, count):
            pivot_row = spread(columns[t][first], u)
            for v in range(first, tiles):
                columns[t][v] = columns[t][v] - factor[v] * pivot_row
        for q in range(parts):
            pivot_row = spread(rows[first][q], u)
            for v in range(first, tiles):
                rows[v][q] = rows[v][q] - factor[v] * pivot_row
    out = []
    for v in range(tiles):
        scale = scales[8 * v]
        for u in range(1, 8):
            scale = jnp.where(sub == u, scales[8 * v + u], scale)
        out.append([part * scale for part in rows[v]])
    return out


def factor_kernel(d, *refs):
    gram_ref, upper, inverse = refs[0], refs[1 : 1 + d], refs[1 + d : 1 + 2 * d]
    upper_ref, inverse_ref, work = refs[1 + 2 * d :]
    rank = gram_ref.shape[1]
    low = BLOCK * d
    here = slice(low, low + BLOCK)
    right = gram_ref[:, low:]
    left = None
    for k in range(d):
        column = upper[k][:, here]
        right = right - exact_dot(column, upper[k][:, low:], ((0,), (0,)))
        term = exact_dot(column, inverse[k][:, :low], ((0,), (0,)))
        left = -term if left is None else left - term
    row_ids = lax.broadcasted_iota(jnp.int32, (BLOCK, BLOCK), 0)
    column_ids = lax.broadcasted_iota(jnp.int32, (BLOCK, BLOCK), 1)
    work[:, :BLOCK] = right[:, :BLOCK]
    work[:, BLOCK:] = (row_ids == column_ids).astype(F32)
    for p in range(0, BLOCK, PIVOTS):
        rows = work[p : p + PIVOTS, :]
        if p:
            rows = rows - exact_dot(work[:p, p : p + PIVOTS], work[:p, :], ((0,), (0,)))
        tiles = [rows[v : v + 8] for v in range(0, PIVOTS, 8)]
        for v, parts in enumerate(eliminate(tiles, p)):
            for q, part in enumerate(parts):
                work[p + 8 * v : p + 8 * v + 8, BLOCK * q : BLOCK * (q + 1)] = part
    block_inverse = work[:, BLOCK:]
    upper_ref[...] = jnp.zeros_like(upper_ref)
    inverse_ref[...] = jnp.zeros_like(inverse_ref)
    upper_ref[:, here] = jnp.where(row_ids <= column_ids, work[:, :BLOCK], 0.0)
    inverse_ref[:, here] = block_inverse
    if low + BLOCK < rank:
        upper_ref[:, low + BLOCK :] = exact_dot(block_inverse, right[:, BLOCK:], ((1,), (0,)))
    if d:
        inverse_ref[:, :low] = exact_dot(block_inverse, left, ((1,), (0,)))


def factor_step(d, gram, upper, inverse):
    rank = gram.shape[1]
    out = jax.ShapeDtypeStruct((BLOCK, rank), F32)
    first = pl.BlockSpec((BLOCK, rank), lambda i: (0, 0))
    return pl.pallas_call(
        functools.partial(factor_kernel, d),
        grid=(1,),
        in_specs=[pl.BlockSpec((BLOCK, rank), lambda i: (d, 0))] + [first] * (2 * d),
        out_specs=(first, first),
        out_shape=(out, out),
        scratch_shapes=[pltpu.VMEM((BLOCK, 2 * BLOCK), F32)],
        compiler_params=params(24),
        cost_estimate=cost(5_000_000_000, 4 * BLOCK * rank * (2 * d + 3)),
        name="factor_step",
    )(gram, *upper, *inverse)


def factorize(gram):
    upper, inverse = [], []
    for d in range(gram.shape[0] // BLOCK):
        up, inv = factor_step(d, gram, upper, inverse)
        upper.append(up)
        inverse.append(inv)
    return jnp.concatenate(upper, 0), jnp.concatenate(inverse, 0)


def shards(panel, sketch_matrix):
    rank = sketch_matrix.shape[1]
    local_rows, local_cols = panel.shape
    total_rows = local_rows * lax.axis_size("row")
    norm_scale = 1.0 / math.sqrt(total_rows)
    row = lax.axis_index("row")
    c = row % CS
    core, y = c.reshape(1), lax.axis_index("col").reshape(1)
    row_share = rank // (ZS * XS * CS)

    with jax.named_scope("sketch"):
        arrived = swap_core(panel)
        pieces = sketch_product(y, panel, sketch_matrix)
        own = place_blocks(y, ring_gather_y(ring_sum_y(*pieces)))
        other = swap_core(own)

    with jax.named_scope("gram"):
        gram, *sketches = gram_product(y, core, own, other)
        gram, *sketches = together(gram, *sketches)
        gram = exchange(gram.reshape(ZS * XS, -1, rank), ZX_GROUPS)

    with jax.named_scope("project"):
        total = project_product(core, sketches, panel, arrived)
        total = lax.psum_scatter(
            total, "row", scatter_dimension=0, axis_index_groups=Z_GROUPS, tiled=True
        )

    with jax.named_scope("gram"):
        gram = exchange(repeat(gram.sum(0), ZS * XS), ZX_GROUPS).reshape(-1, rank)
        gram = place_blocks(y, ring_gather_y(gram)).reshape(YS, -1, rank)
        gram = place({0: gram, 1: swap_core(gram)}, CS, c)
        gram = gram.transpose(1, 0, 2, 3).reshape(rank, rank)

    with jax.named_scope("factor"):
        upper, inverse = factorize(gram)

    with jax.named_scope("apply"):
        result = lax.dot_general(
            inverse,
            total,
            (((1,), (1,)), ((), ())),
            precision=lax.Precision.HIGH,
            preferred_element_type=F32,
        )
        width = result.shape[1]
        result = exchange(result.reshape(-1, row_share, width), None)
        result = result.reshape(ZS, XS, CS, row_share, width).sum(1) * norm_scale
        projected = result.transpose(2, 1, 0, 3).reshape(row_share, local_cols)
        spread = lax.dynamic_slice_in_dim(upper, row * row_share, row_share, 0) * norm_scale
    return (projected, spread)


def solution(mesh):
    return jax.shard_map(
        shards,
        mesh=mesh,
        in_specs=(P("row", "col"), P("col", None)),
        out_specs=(P("row", "col"), P("row", None)),
        check_vma=False,
    )
```

time: 649 us -> 177 us (0.27)
  waiting for transfers between devices: 438 us -> 41.8 us
  other arithmetic: 126 us -> 2.78 us
  Pallas kernels: 0 us -> 44 us
  matrix products: 45.9 us -> 2.46 us
  starting transfers between devices: 0.59 us -> 33.9 us
  blocking collectives: 0 us -> 33.1 us
  local copies, waits for them, and re-layouts: 16.1 us -> 4.51 us
    psum x2 -> x0, waiting for transfers between devices: 239 us -> none  [the longest x1 185 us: shards(): gram_sum = lax.psum(inner_rows(own_rows, own_rows), 'row')]
    unnamed x4 -> x1, waiting for transfers between devices: 199 us -> 0.02 us
    another operation x17 -> x0, other arithmetic: 122 us -> none  [the longest x14 80.2 us: shards(): lower_factor = jnp.linalg.cholesky(gram_sum)]
    pallas_call x0 -> x9, Pallas kernels: none -> 44 us  [the longest x4 19.8 us: factor_step(): pl.pallas_call(functools.partial(factor_kernel, d), grid=(1,), in_specs=[...]
    dot_general x3 -> x1, matrix products: 39 us -> 2.46 us  [shards(): lax.dot_general(inverse, total, (((1,), (1,)), ((), ())), precision=lax.P...]
    all_to_all x0 -> x2, blocking collectives: none -> 33.1 us  [exchange(): return lax.all_to_all(array, 'row', 0, 0, axis_index_groups=groups)]
    ppermute x0 -> x15, starting transfers between devices: none -> 29.4 us  [the longest x12 17 us: send_y(): return lax.ppermute(array, 'col', [(i, (i + step) % YS) for i in range(YS)])]
    ppermute x0 -> x15, waiting for transfers between devices: none -> 24.6 us  [the longest x12 20.9 us: send_y(): return lax.ppermute(array, 'col', [(i, (i + step) % YS) for i in range(YS)])]
  transfers between devices with their start and end apart: 3 -> 17, of which waited for: 3 -> 9; matrix products, arithmetic and copies ran while one was open for 0% -> 2% of each run, Pallas kernels for 0% -> 18%
where the time goes in v1:
time: 177 us
  Pallas kernels  44 us (25%)
  waiting for transfers between devices  41.8 us (24%)
  starting transfers between devices  33.9 us (19%)
  blocking collectives  33.1 us (19%)
  between operations  14.2 us (8%)
  local copies, waits for them, and re-layouts  4.51 us (3%)
  other arithmetic  2.78 us (2%)
  matrix products  2.46 us (1%)
    all_to_all x2, blocking collectives, exchange(): return lax.all_to_all(array, 'row', 0, 0, axis_index_groups=groups)  33.1 us
    ppermute x12, waiting for transfers between devices, send_y(): return lax.ppermute(array, 'col', [(i, (i + step) % YS) for i in range(YS)])  20.9 us
    pallas_call x4, Pallas kernels, factor_step(): pl.pallas_call(functools.partial(factor_kernel, d), grid=(1,), in_specs=[...  19.8 us
    all_to_all x1, waiting for transfers between devices, exchange(): return lax.all_to_all(array, 'row', 0, 0, axis_index_groups=groups)  17.2 us
    ppermute x12, starting transfers between devices, send_y(): return lax.ppermute(array, 'col', [(i, (i + step) % YS) for i in range(YS)])  17 us
    ppermute x3, starting transfers between devices, swap_core(): return lax.ppermute(array, 'row', row_pairs(lambda z, x, c: (z, x, 1 - c)))  12.4 us
    pallas_call x1, Pallas kernels, project_product(): pl.pallas_call(project_kernel, in_specs=[IN_SMEM] + [IN_PLACE] * 6, out_s...  11.9 us
    pallas_call x1, Pallas kernels, sketch_product(): pl.pallas_call(sketch_kernel, in_specs=[IN_SMEM, IN_PLACE, IN_PLACE], out...  10.8 us
  transfers between devices with their start and end apart: 17, of which 9 were waited for; matrix products, arithmetic and copies ran while one was open for 2% of the time, Pallas kernels for 18%

profile of v1, /device:TPU:1, one launch (start us, length us, event | category | flops | bytes accessed | tf_op | source)
XLA Modules:
  0.0 176.9 jit_solution(16979309778064720821)
XLA Ops:
  7.2 3.3 %collective-permute-start.14 = (f32[512,4096]{1,0:T(8,128)}, f32[512,4096]{1,0:T(8,128)}, u32[]{:S(2)}, u32[]{:S(2)}) collective-permute-start(f32[512,4096]{1,0:T(8,128)} %panel_ref.3), channel_id=1, source_target_pairs={{0,4},{4,0},{8,12},{12,8},{16,20},{20,16},{24,28},{28,24},{32,36},... | collective-permute-start | bytes 25165832 | tf_op jit(solution)/shard_map/sketch/ppermute | solution.py:40
  10.5 10.8 %sketch_product.1 = (f32[128,512]{1,0:T(8,128)}, f32[128,512]{1,0:T(8,128)}, f32[64,512]{1,0:T(8,128)}, f32[64,512]{1,0:T(8,128)}, f32[128,512]{1,0:T(8,128)}) custom-call(s32[1]{0:T(128)} %bitcast.y_ref, f32[512,4096]{1,0:T(8,128)} %panel_ref.3, f32[4096,512]{1,0:T(8,128)} %matrix_ref.1), custom_call_target="tpu_custom_call" | custom-call | flops 6442450944 | bytes 16777216 | tf_op jit(solution)/shard_map/sketch/sketch_product/pallas_call | solution.py:151
  21.4 2.7 %collective-permute-start.1 = (f32[128,512]{1,0:T(8,128)}, f32[128,512]{1,0:T(8,128)S(1)}, u32[]{:S(2)}, u32[]{:S(2)}) collective-permute-start(f32[128,512]{1,0:T(8,128)} %get-tuple-element.32), channel_id=1, source_target_pairs={{0,3},{1,0},{2,1},{3,2},{4,7},{5,4},{6,5},{7,6},{8,11},{9,8},{10,9... | collective-permute-start | bytes 786440 | tf_op jit(solution)/shard_map/sketch/ppermute | solution.py:36
  24.1 6.7 %collective-permute-done = f32[128,512]{1,0:T(8,128)S(1)} collective-permute-done((f32[128,512]{1,0:T(8,128)}, f32[128,512]{1,0:T(8,128)S(1)}, u32[]{:S(2)}, u32[]{:S(2)}) %collective-permute-start) | collective-permute-done | bytes 262176 | tf_op jit(solution)/shard_map/sketch/ppermute | solution.py:36
  31.8 2.7 %collective-permute-start.3 = (f32[64,512]{1,0:T(8,128)S(1)}, f32[64,512]{1,0:T(8,128)S(1)}, u32[]{:S(2)}, u32[]{:S(2)}) collective-permute-start(f32[64,512]{1,0:T(8,128)S(1)} %get-tuple-element.38), channel_id=1, source_target_pairs={{0,3},{1,0},{2,1},{3,2},{4,7},{5,4},{6,5},{7,6},{8,11},{9,8},{10,9... | collective-permute-start | bytes 393224 | tf_op jit(solution)/shard_map/sketch/ppermute | solution.py:36
  34.5 2.8 %collective-permute-done.2 = f32[64,512]{1,0:T(8,128)S(1)} collective-permute-done((f32[64,512]{1,0:T(8,128)S(1)}, f32[64,512]{1,0:T(8,128)S(1)}, u32[]{:S(2)}, u32[]{:S(2)}) %collective-permute-start.2) | collective-permute-done | bytes 131104 | tf_op jit(solution)/shard_map/sketch/ppermute | solution.py:36
  38.5 2.5 %collective-permute-start.5 = (f32[128,512]{1,0:T(8,128)S(1)}, f32[128,512]{1,0:T(8,128)S(1)}, u32[]{:S(2)}, u32[]{:S(2)}) collective-permute-start(f32[128,512]{1,0:T(8,128)S(1)} %maximum_add_fusion.own), channel_id=1, source_target_pairs={{0,3},{1,0},{2,1},{3,2},{4,7},{5,4},{6,5},{7,6},{8,11},{9,8},{10,9... | collective-permute-start | bytes 786440 | tf_op jit(solution)/shard_map/sketch/ppermute | solution.py:36
  41.1 4.6 %collective-permute-done.4.before = f32[128,512]{1,0:T(8,128)S(1)} collective-permute-done((f32[128,512]{1,0:T(8,128)S(1)}, f32[128,512]{1,0:T(8,128)S(1)}, u32[]{:S(2)}, u32[]{:S(2)}) %collective-permute-start.4) | collective-permute-done | bytes 262176 | tf_op jit(solution)/shard_map/sketch/ppermute | solution.py:36
  45.8 2.7 %collective-permute-start.7 = (f32[64,512]{1,0:T(8,128)S(1)}, f32[64,512]{1,0:T(8,128)S(1)}, u32[]{:S(2)}, u32[]{:S(2)}) collective-permute-start(f32[64,512]{1,0:T(8,128)S(1)} %slice.29), channel_id=1, source_target_pairs={{0,3},{1,0},{2,1},{3,2},{4,7},{5,4},{6,5},{7,6},{8,11},{9,8},{10,9... | collective-permute-start | bytes 393224 | tf_op jit(solution)/shard_map/sketch/ppermute | solution.py:36
  48.6 2.3 %collective-permute-done.6.head = f32[64,512]{1,0:T(8,128)S(1)} collective-permute-done((f32[64,512]{1,0:T(8,128)S(1)}, f32[64,512]{1,0:T(8,128)S(1)}, u32[]{:S(2)}, u32[]{:S(2)}) %collective-permute-start.6) | collective-permute-done | bytes 131104 | tf_op jit(solution)/shard_map/sketch/ppermute | solution.py:36
  50.9 3.9 %collective-permute-start.8 = (f32[512,512]{1,0:T(8,128)S(1)}, f32[512,512]{1,0:T(8,128)S(1)}, u32[]{:S(2)}, u32[]{:S(2)}) collective-permute-start(f32[512,512]{1,0:T(8,128)S(1)} %bitcast.25), channel_id=1, source_target_pairs={{0,4},{4,0},{8,12},{12,8},{16,20},{20,16},{24,28},{28,24},{32,36},... | collective-permute-start | bytes 3145736 | tf_op jit(solution)/shard_map/sketch/ppermute | solution.py:40
  54.8 2.3 %collective-permute-done.8.other_ref = f32[512,512]{1,0:T(8,128)S(1)} collective-permute-done((f32[512,512]{1,0:T(8,128)S(1)}, f32[512,512]{1,0:T(8,128)S(1)}, u32[]{:S(2)}, u32[]{:S(2)}) %collective-permute-start.8) | collective-permute-done | bytes 1048608 | tf_op jit(solution)/shard_map/sketch/ppermute | solution.py:40
  61.8 11.9 %project_product.1 = f32[2048,512]{1,0:T(8,128)} custom-call(s32[1]{0:T(128)} %bitcast.1.core_ref, bf16[512,512]{1,0:T(8,128)(2,1)} %copy-done, bf16[512,512]{1,0:T(8,128)(2,1)} %copy-done.1, bf16[512,512]{1,0:T(8,128)(2,1)} %copy-done.2, bf16[512,512]{1,0:T(8,128)(2,1)} %copy-done.3, f32[512,4096]{1,0:T(8,128)} %panel_ref.3, ...), custom_call_target="tpu_custom_call" | custom-call | flops 6442450944 | bytes 25165824 | tf_op jit(solution)/shard_map/project/project_product/pallas_call | solution.py:286
  73.8 18.6 %all_to_all.15 = f32[32,2,512]{2,1,0:T(2,128)S(1)} all-to-all(f32[32,2,512]{2,1,0:T(2,128)S(1)} %reshape.35), channel_id=1, replica_groups={{0,8,16,24,32,40,48,56,64,72,80,88,96,104,112,120,128,136,144,152,160,1..., dimensions={0} | all-to-all | bytes 262144 | tf_op jit(solution)/shard_map/gram/all_to_all | solution.py:44
  92.5 14.5 %all_to_all.16 = f32[32,2,512]{2,1,0:T(2,128)S(1)} all-to-all(f32[32,2,512]{2,1,0:T(2,128)S(1)} %broadcast_in_dim.17), channel_id=1, replica_groups={{0,8,16,24,32,40,48,56,64,72,80,88,96,104,112,120,128,136,144,152,160,1..., dimensions={0} | all-to-all | bytes 262144 | tf_op jit(solution)/shard_map/gram/all_to_all | solution.py:44
  110.3 2.7 %collective-permute-done.9.before = f32[64,512]{1,0:T(8,128)S(1)} collective-permute-done((f32[64,512]{1,0:T(8,128)S(1)}, f32[64,512]{1,0:T(8,128)S(1)}, u32[]{:S(2)}, u32[]{:S(2)}) %collective-permute-start.9) | collective-permute-done | bytes 131104 | tf_op jit(solution)/shard_map/gram/ppermute | solution.py:36
  117.8 5.2 %collective-permute-start.13 = (f32[4,64,512]{2,1,0:T(8,128)S(1)}, f32[4,64,512]{2,1,0:T(8,128)S(1)}, u32[]{:S(2)}, u32[]{:S(2)}) collective-permute-start(f32[4,64,512]{2,1,0:T(8,128)S(1)} %place_blocks.3), channel_id=1, source_target_pairs={{0,4},{4,0},{8,12},{12,8},{16,20},{20,16},{24,28},{28,24},{32,36},... | collective-permute-start | bytes 1572872 | tf_op jit(solution)/shard_map/gram/ppermute | solution.py:40
  124.6 4.5 %factor_step.4 = (f32[128,512]{1,0:T(8,128)S(1)}, f32[128,512]{1,0:T(8,128)S(1)}) custom-call(f32[512,512]{1,0:T(8,128)S(1)} %bitcast.27), custom_call_target="tpu_custom_call" | custom-call | flops 5000000000 | bytes 786432 | tf_op jit(solution)/shard_map/factor/factor_step/pallas_call | solution.py:390
  129.1 4.8 %factor_step.5 = (f32[128,512]{1,0:T(8,128)S(1)}, f32[128,512]{1,0:T(8,128)S(1)}) custom-call(f32[512,512]{1,0:T(8,128)S(1)} %bitcast.28, f32[128,512]{1,0:T(8,128)S(1)} %get-tuple-element.47.refs_1_, f32[128,512]{1,0:T(8,128)S(1)} %get-tuple-element.46.refs_2_.refs_3_.refs_4_), custom_call_target="tpu_custom_call" | custom-call | flops 5000000000 | bytes 1310720 | tf_op jit(solution)/shard_map/factor/factor_step/pallas_call | solution.py:390
  134.0 5.0 %factor_step.6 = (f32[128,512]{1,0:T(8,128)S(1)}, f32[128,512]{1,0:T(8,128)S(1)}) custom-call(f32[512,512]{1,0:T(8,128)S(1)} %bitcast.29, f32[128,512]{1,0:T(8,128)S(1)} %get-tuple-element.47.refs_1_, f32[128,512]{1,0:T(8,128)S(1)} %get-tuple-element.49.refs_2_, f32[128,512]{1,0:T(8,128)S(1)} %get-tuple-element.46.refs_2_.refs_3_.refs_4_, ...), custom_call_target="tpu_custom_call" | custom-call | flops 5000000000 | bytes 1835008 | tf_op jit(solution)/shard_map/factor/factor_step/pallas_call | solution.py:390
  139.0 5.4 %factor_step.7 = (f32[128,512]{1,0:T(8,128)S(1)}, f32[128,512]{1,0:T(8,128)S(1)}) custom-call(f32[512,512]{1,0:T(8,128)S(1)} %bitcast.30, f32[128,512]{1,0:T(8,128)S(1)} %get-tuple-element.47.refs_1_, f32[128,512]{1,0:T(8,128)S(1)} %get-tuple-element.49.refs_2_, f32[128,512]{1,0:T(8,128)S(1)} %get-tuple-element.51.refs_3_, ...), custom_call_target="tpu_custom_call" | custom-call | flops 5000000000 | bytes 2359296 | tf_op jit(solution)/shard_map/factor/factor_step/pallas_call | solution.py:390
  144.4 2.5 %convolution_bitcast_fusion = f32[64,8,256]{2,1,0:T(8,128)} fusion(f32[256,512]{1,0:T(8,128)} %reduce-scatter.2.cloned.1.call-done, f32[128,512]{1,0:T(8,128)S(1)} %get-tuple-element.52, f32[128,512]{1,0:T(8,128)S(1)} %get-tuple-element.50.refs_6_, f32[128,512]{1,0:T(8,128)S(1)} %get-tuple-element.48.refs_4_.refs_5_, ...), kind=kOutput, calls=%fused_computation | convolution fusion | flops 403439616 | bytes 2097152 | tf_op jit(solution)/shard_map/apply/dot_general | solution.py:449
  146.9 4.4 %all-to-all-start.2 = ((f32[64,8,256]{2,1,0:T(8,128)}), f32[64,8,256]{2,1,0:T(8,128)S(1)}, u32[]{:S(2)}, u32[]{:S(2)}) async-start(f32[64,8,256]{2,1,0:T(8,128)} %convolution_bitcast_fusion), calls=%async_computation.3 | async-start | bytes 1048576 | tf_op jit(solution)/shard_map/apply/all_to_all | solution.py:44
  152.0 17.2 %all-to-all-done.2 = f32[64,8,256]{2,1,0:T(8,128)S(1)} async-done(((f32[64,8,256]{2,1,0:T(8,128)}), f32[64,8,256]{2,1,0:T(8,128)S(1)}, u32[]{:S(2)}, u32[]{:S(2)}) %all-to-all-start.2) | async-done | bytes 524320 | tf_op jit(solution)/shard_map/apply/all_to_all | solution.py:44
  (51 shorter events, 18.7 us)
Async XLA Ops:
  7.2 137.3 %reduce-scatter.2.cloned.1.call-start = ((), (), s32[]{:S(2)}) async-start(), calls=%async_computation.4 | async-start | bytes 4718592 | tf_op jit(solution)/shard_map/project/reduce_scatter | solution.py:435
  7.2 54.6 %collective-permute-start.14 = (f32[512,4096]{1,0:T(8,128)}, f32[512,4096]{1,0:T(8,128)}, u32[]{:S(2)}, u32[]{:S(2)}) collective-permute-start(f32[512,4096]{1,0:T(8,128)} %panel_ref.3), channel_id=1, source_target_pairs={{0,4},{4,0},{8,12},{12,8},{16,20},{20,16},{24,28},{28,24},{32,36},... | collective-permute-start | bytes 25165832 | tf_op jit(solution)/shard_map/sketch/ppermute | solution.py:40
  21.3 9.4 %collective-permute-start = (f32[128,512]{1,0:T(8,128)}, f32[128,512]{1,0:T(8,128)S(1)}, u32[]{:S(2)}, u32[]{:S(2)}) collective-permute-start(f32[128,512]{1,0:T(8,128)} %get-tuple-element.31), channel_id=1, source_target_pairs={{0,1},{1,2},{2,3},{3,0},{4,5},{5,6},{6,7},{7,4},{8,9},{9,10},{10,1... | collective-permute-start | bytes 786440 | tf_op jit(solution)/shard_map/sketch/ppermute | solution.py:36
  21.4 9.3 %collective-permute-start.1 = (f32[128,512]{1,0:T(8,128)}, f32[128,512]{1,0:T(8,128)S(1)}, u32[]{:S(2)}, u32[]{:S(2)}) collective-permute-start(f32[128,512]{1,0:T(8,128)} %get-tuple-element.32), channel_id=1, source_target_pairs={{0,3},{1,0},{2,1},{3,2},{4,7},{5,4},{6,5},{7,6},{8,11},{9,8},{10,9... | collective-permute-start | bytes 786440 | tf_op jit(solution)/shard_map/sketch/ppermute | solution.py:36
  31.8 5.5 %collective-permute-start.2 = (f32[64,512]{1,0:T(8,128)S(1)}, f32[64,512]{1,0:T(8,128)S(1)}, u32[]{:S(2)}, u32[]{:S(2)}) collective-permute-start(f32[64,512]{1,0:T(8,128)S(1)} %get-tuple-element.37), channel_id=1, source_target_pairs={{0,1},{1,2},{2,3},{3,0},{4,5},{5,6},{6,7},{7,4},{8,9},{9,10},{10,1... | collective-permute-start | bytes 393224 | tf_op jit(solution)/shard_map/sketch/ppermute | solution.py:36
  31.8 5.4 %collective-permute-start.3 = (f32[64,512]{1,0:T(8,128)S(1)}, f32[64,512]{1,0:T(8,128)S(1)}, u32[]{:S(2)}, u32[]{:S(2)}) collective-permute-start(f32[64,512]{1,0:T(8,128)S(1)} %get-tuple-element.38), channel_id=1, source_target_pairs={{0,3},{1,0},{2,1},{3,2},{4,7},{5,4},{6,5},{7,6},{8,11},{9,8},{10,9... | collective-permute-start | bytes 393224 | tf_op jit(solution)/shard_map/sketch/ppermute | solution.py:36
  38.3 7.4 %collective-permute-start.4 = (f32[128,512]{1,0:T(8,128)S(1)}, f32[128,512]{1,0:T(8,128)S(1)}, u32[]{:S(2)}, u32[]{:S(2)}) collective-permute-start(f32[128,512]{1,0:T(8,128)S(1)} %maximum_add_fusion.own), channel_id=1, source_target_pairs={{0,1},{1,2},{2,3},{3,0},{4,5},{5,6},{6,7},{7,4},{8,9},{9,10},{10,1... | collective-permute-start | bytes 786440 | tf_op jit(solution)/shard_map/sketch/ppermute | solution.py:36
  38.5 7.2 %collective-permute-start.5 = (f32[128,512]{1,0:T(8,128)S(1)}, f32[128,512]{1,0:T(8,128)S(1)}, u32[]{:S(2)}, u32[]{:S(2)}) collective-permute-start(f32[128,512]{1,0:T(8,128)S(1)} %maximum_add_fusion.own), channel_id=1, source_target_pairs={{0,3},{1,0},{2,1},{3,2},{4,7},{5,4},{6,5},{7,6},{8,11},{9,8},{10,9... | collective-permute-start | bytes 786440 | tf_op jit(solution)/shard_map/sketch/ppermute | solution.py:36
  45.7 5.1 %collective-permute-start.6 = (f32[64,512]{1,0:T(8,128)S(1)}, f32[64,512]{1,0:T(8,128)S(1)}, u32[]{:S(2)}, u32[]{:S(2)}) collective-permute-start(f32[64,512]{1,0:T(8,128)S(1)} %slice.28), channel_id=1, source_target_pairs={{0,1},{1,2},{2,3},{3,0},{4,5},{5,6},{6,7},{7,4},{8,9},{9,10},{10,1... | collective-permute-start | bytes 393224 | tf_op jit(solution)/shard_map/sketch/ppermute | solution.py:36
  45.8 5.0 %collective-permute-start.7 = (f32[64,512]{1,0:T(8,128)S(1)}, f32[64,512]{1,0:T(8,128)S(1)}, u32[]{:S(2)}, u32[]{:S(2)}) collective-permute-start(f32[64,512]{1,0:T(8,128)S(1)} %slice.29), channel_id=1, source_target_pairs={{0,3},{1,0},{2,1},{3,2},{4,7},{5,4},{6,5},{7,6},{8,11},{9,8},{10,9... | collective-permute-start | bytes 393224 | tf_op jit(solution)/shard_map/sketch/ppermute | solution.py:36
  50.9 6.2 %collective-permute-start.8 = (f32[512,512]{1,0:T(8,128)S(1)}, f32[512,512]{1,0:T(8,128)S(1)}, u32[]{:S(2)}, u32[]{:S(2)}) collective-permute-start(f32[512,512]{1,0:T(8,128)S(1)} %bitcast.25), channel_id=1, source_target_pairs={{0,4},{4,0},{8,12},{12,8},{16,20},{20,16},{24,28},{28,24},{32,36},... | collective-permute-start | bytes 3145736 | tf_op jit(solution)/shard_map/sketch/ppermute | solution.py:40
  58.6 0.9 copy-start
  59.4 0.8 copy-start.1
  60.2 0.8 copy-start.2
  61.0 0.8 copy-start.3
  107.2 5.8 %collective-permute-start.9 = (f32[64,512]{1,0:T(8,128)S(1)}, f32[64,512]{1,0:T(8,128)S(1)}, u32[]{:S(2)}, u32[]{:S(2)}) collective-permute-start(f32[64,512]{1,0:T(8,128)S(1)} %reshape.36.own), channel_id=1, source_target_pairs={{0,1},{1,2},{2,3},{3,0},{4,5},{5,6},{6,7},{7,4},{8,9},{9,10},{10,1... | collective-permute-start | bytes 393224 | tf_op jit(solution)/shard_map/gram/ppermute | solution.py:36
  108.4 4.5 %collective-permute-start.10 = (f32[64,512]{1,0:T(8,128)S(1)}, f32[64,512]{1,0:T(8,128)S(1)}, u32[]{:S(2)}, u32[]{:S(2)}) collective-permute-start(f32[64,512]{1,0:T(8,128)S(1)} %reshape.36.own), channel_id=1, source_target_pairs={{0,3},{1,0},{2,1},{3,2},{4,7},{5,4},{6,5},{7,6},{8,11},{9,8},{10,9... | collective-permute-start | bytes 393224 | tf_op jit(solution)/shard_map/gram/ppermute | solution.py:36
  113.0 4.8 %collective-permute-start.11 = (f32[32,512]{1,0:T(8,128)S(1)}, f32[32,512]{1,0:T(8,128)S(1)}, u32[]{:S(2)}, u32[]{:S(2)}) collective-permute-start(f32[32,512]{1,0:T(8,128)S(1)} %slice.30), channel_id=1, source_target_pairs={{0,1},{1,2},{2,3},{3,0},{4,5},{5,6},{6,7},{7,4},{8,9},{9,10},{10,1... | collective-permute-start | bytes 196616 | tf_op jit(solution)/shard_map/gram/ppermute | solution.py:36
  114.2 3.6 %collective-permute-start.12 = (f32[32,512]{1,0:T(8,128)S(1)}, f32[32,512]{1,0:T(8,128)S(1)}, u32[]{:S(2)}, u32[]{:S(2)}) collective-permute-start(f32[32,512]{1,0:T(8,128)S(1)} %slice.31), channel_id=1, source_target_pairs={{0,3},{1,0},{2,1},{3,2},{4,7},{5,4},{6,5},{7,6},{8,11},{9,8},{10,9... | collective-permute-start | bytes 196616 | tf_op jit(solution)/shard_map/gram/ppermute | solution.py:36
  117.8 6.7 %collective-permute-start.13 = (f32[4,64,512]{2,1,0:T(8,128)S(1)}, f32[4,64,512]{2,1,0:T(8,128)S(1)}, u32[]{:S(2)}, u32[]{:S(2)}) collective-permute-start(f32[4,64,512]{2,1,0:T(8,128)S(1)} %place_blocks.3), channel_id=1, source_target_pairs={{0,4},{4,0},{8,12},{12,8},{16,20},{20,16},{24,28},{28,24},{32,36},... | collective-permute-start | bytes 1572872 | tf_op jit(solution)/shard_map/gram/ppermute | solution.py:40
  146.9 22.3 %all-to-all-start.2 = ((f32[64,8,256]{2,1,0:T(8,128)}), f32[64,8,256]{2,1,0:T(8,128)S(1)}, u32[]{:S(2)}, u32[]{:S(2)}) async-start(f32[64,8,256]{2,1,0:T(8,128)} %convolution_bitcast_fusion), calls=%async_computation.3 | async-start | bytes 1048576 | tf_op jit(solution)/shard_map/apply/all_to_all | solution.py:44
Sparse Core Ops, SparseCore 0:
  73.9 59.9 reduce-scatter.1

commit v2 on v1

--- a/solution.py
+++ b/solution.py
@@ -100,18 +100,26 @@
 IN_SMEM = pl.BlockSpec(memory_space=pltpu.SMEM)
 
 
-def sketch_kernel(
-    y_ref, panel_ref, matrix_ref, ahead_ref, behind_ref, next_ref, before_ref, own_ref,
-    panels, matrices, total, panel_sems, matrix_sems,
-):
+def sketch_kernel(pieces, y_ref, panel_ref, matrix_ref, *refs):
+    out_refs, (panels, matrices, total, panel_sems, matrix_sems) = refs[:-5], refs[-5:]
     steps, _, width = panels.shape
+    block = panel_ref.shape[0] // YS
 
     def copies(k):
         at = pl.ds(pl.multiple_of(k * width, width), width)
-        return (
-            pltpu.make_async_copy(panel_ref.at[:, at], panels.at[k], panel_sems.at[k]),
-            pltpu.make_async_copy(matrix_ref.at[at], matrices.at[k], matrix_sems.at[k]),
-        )
+        out = [pltpu.make_async_copy(matrix_ref.at[at], matrices.at[k], matrix_sems.at[k])]
+        offset = 0
+        for i, (step, start, size) in enumerate(pieces):
+            row = lax.rem(y_ref[0] + step, YS) * block + start
+            out.append(
+                pltpu.make_async_copy(
+                    panel_ref.at[pl.ds(pl.multiple_of(row, block // 2), size), at],
+                    panels.at[k, pl.ds(offset, size)],
+                    panel_sems.at[k, i],
+                )
+            )
+            offset += size
+        return out
 
     for k in range(steps):
         for copy in copies(k):
@@ -125,39 +133,28 @@
         return carry
 
     lax.fori_loop(0, steps, step, 0)
-    block = own_ref.shape[0]
-    half = block // 2
-
-    def rows(step, start, size):
-        at = lax.rem(y_ref[0] + step, YS) * block + start
-        return total[pl.ds(pl.multiple_of(at, half), size), :]
-
-    ahead_ref[:half] = rows(2, 0, half)
-    ahead_ref[half:] = rows(1, half, half)
-    behind_ref[:half] = rows(3, 0, half)
-    behind_ref[half:] = rows(2, half, half)
-    next_ref[...] = rows(1, 0, half)
-    before_ref[...] = rows(3, half, half)
-    own_ref[...] = rows(0, 0, block)
-
-
-def sketch_product(y, panel, matrix):
-    rows, depth = panel.shape
+    offset = 0
+    for out_ref in out_refs:
+        size = out_ref.shape[0]
+        out_ref[...] = total[offset : offset + size]
+        offset += size
+
+
+def sketch_product(y, panel, matrix, pieces, sizes):
+    depth = panel.shape[1]
+    rows = sum(sizes)
     rank = matrix.shape[1]
     steps = depth // WIDTH
-    block = rows // YS
-    whole = jax.ShapeDtypeStruct((block, rank), F32)
-    half = jax.ShapeDtypeStruct((block // 2, rank), F32)
     return pl.pallas_call(
-        sketch_kernel,
+        functools.partial(sketch_kernel, pieces),
         in_specs=[IN_SMEM, IN_PLACE, IN_PLACE],
-        out_specs=(IN_VMEM,) * 5,
-        out_shape=(whole, whole, half, half, whole),
+        out_specs=(IN_VMEM,) * len(sizes),
+        out_shape=tuple(jax.ShapeDtypeStruct((size, rank), F32) for size in sizes),
         scratch_shapes=[
             pltpu.VMEM((steps, rows, WIDTH), F32),
             pltpu.VMEM((steps, WIDTH, rank), F32),
             pltpu.VMEM((rows, rank), F32),
-            pltpu.SemaphoreType.DMA((steps,)),
+            pltpu.SemaphoreType.DMA((steps, len(pieces))),
             pltpu.SemaphoreType.DMA((steps,)),
         ],
         compiler_params=params(54),
@@ -166,15 +163,15 @@
     )(y, panel, matrix)
 
 
-def place_kernel(y_ref, own, before, after, head, tail, out_ref):
+def place_kernel(y_ref, own, before, after, head, tail, placed):
     y = y_ref[0]
     at = lambda step: lax.rem(y + step, YS)
-    half = out_ref.shape[1] // 2
-    out_ref[at(0)] = own[...]
-    out_ref[at(3)] = before[...]
-    out_ref[at(1)] = after[...]
-    out_ref[at(2), :half] = head[...]
-    out_ref[at(2), half:] = tail[...]
+    half = placed.shape[1] // 2
+    placed[at(0)] = own[...]
+    placed[at(3)] = before[...]
+    placed[at(1)] = after[...]
+    placed[at(2), :half] = head[...]
+    placed[at(2), half:] = tail[...]
 
 
 def place_blocks(y, blocks):
@@ -184,61 +181,15 @@
         in_specs=[IN_SMEM] + [IN_VMEM] * 5,
         out_specs=IN_VMEM,
         out_shape=jax.ShapeDtypeStruct((YS, rows, rank), F32),
-        compiler_params=params(16),
+        compiler_params=params(24),
         cost_estimate=cost(0, 8 * YS * rows * rank),
         name="place_blocks",
     )(y, *blocks).reshape(YS * rows, rank)
 
 
-def gram_kernel(
-    y_ref, core_ref, own_ref, other_ref, gram_ref, own_high, own_low, other_high, other_low,
-    parts, turned, sems,
-):
-    outs = (own_high, own_low, other_high, other_low)
-    leave = lambda k: pltpu.make_async_copy(parts.at[k], outs[k], sems.at[k])
-    share = gram_ref.shape[0]
-    total = None
-    for k, sketch_ref in enumerate((own_ref, other_ref)):
-        sketch = sketch_ref[...]
-        high, low = split(sketch)
-        parts[2 * k] = high
-        parts[2 * k + 1] = low
-        leave(2 * k).start()
-        leave(2 * k + 1).start()
-        block = CS * share
-        columns = pl.ds(pl.multiple_of(y_ref[0] * block, block), block)
-        turned[...] = sketch_ref[:, columns].T
-        rows = turned[pl.ds(pl.multiple_of(core_ref[0] * share, share), share), :]
-        term = dot_parts(split(rows), (high, low))
-        total = term if total is None else total + term
-    gram_ref[...] = total
-    for k in range(4):
-        leave(k).wait()
-
-
-def gram_product(y, core, own, other):
-    rows, rank = own.shape
-    share = rank // (YS * CS)
-    part = jax.ShapeDtypeStruct((rows, rank), BF16)
-    return pl.pallas_call(
-        gram_kernel,
-        in_specs=[IN_SMEM, IN_SMEM, IN_VMEM, IN_VMEM],
-        out_specs=(IN_VMEM,) + (IN_PLACE,) * 4,
-        out_shape=(jax.ShapeDtypeStruct((share, rank), F32),) + (part,) * 4,
-        scratch_shapes=[
-            pltpu.VMEM((4, rows, rank), BF16),
-            pltpu.VMEM((CS * share, rows), F32),
-            pltpu.SemaphoreType.DMA((4,)),
-        ],
-        compiler_params=params(24),
-        cost_estimate=cost(12 * rows * rank * share, 16 * rows * rank),
-        name="gram_product",
-    )(y, core, own, other)
-
-
-def project_kernel(
-    core_ref, own_high, own_low, other_high, other_low, panel_ref, arrived_ref, out_ref,
-    sketches, panels, arrived, outs, sketch_sems, panel_sems, arrived_sems, out_sems,
+def chip_kernel(
+    y_ref, core_ref, own_ref, other_ref, panel_ref, arrived_ref, gram_ref, out_ref,
+    parts, turned, gram, panels, arrived, outs, panel_sems, arrived_sems, out_sems,
 ):
     steps, _, width = panels.shape
     base = core_ref[0] * (steps * width)
@@ -254,23 +205,32 @@
         at = pl.ds(pl.multiple_of(k * width, width), width)
         return pltpu.make_async_copy(outs.at[k], out_ref.at[at], out_sems.at[k])
 
-    loads = [
-        pltpu.make_async_copy(part, sketches.at[k], sketch_sems.at[k])
-        for k, part in enumerate((own_high, own_low, other_high, other_low))
-    ]
-    for copy in loads:
-        copy.start()
     for k in range(steps):
         for copy in arrive(k):
             copy.start()
-    for copy in loads:
-        copy.wait()
+    share = gram.shape[0]
+    block = CS * share
+    columns = pl.ds(pl.multiple_of(y_ref[0] * block, block), block)
+    for k, sketch_ref in enumerate((own_ref, other_ref)):
+        high, low = split(sketch_ref[...])
+        parts[2 * k] = high
+        parts[2 * k + 1] = low
+        turned[...] = sketch_ref[:, columns].T
+        rows = turned[pl.ds(pl.multiple_of(core_ref[0] * share, share), share), :]
+        term = dot_parts(split(rows), (high, low))
+        if k == 0:
+            gram[...] = term
+        else:
+            gram[...] += term
+    size = gram_ref.shape[1]
+    for k in range(gram_ref.shape[0]):
+        gram_ref[k] = gram[size * k : size * (k + 1), :]
 
     def step(k, carry):
         for copy in arrive(k):
             copy.wait()
-        own = dot_parts(split(panels[k].T), (sketches[0], sketches[1]))
-        outs[k] = own + dot_parts(split(arrived[k].T), (sketches[2], sketches[3]))
+        own = dot_parts(split(panels[k].T), (parts[0], parts[1]))
+        outs[k] = own + dot_parts(split(arrived[k].T), (parts[2], parts[3]))
         leave(k).start()
         return carry
 
@@ -279,29 +239,34 @@
         leave(k).wait()
 
 
-def project_product(core, sketches, panel, arrived):
-    rows, rank = sketches[0].shape
+def chip_products(y, core, own, other, panel, arrived):
+    rows, rank = own.shape
+    share = rank // (YS * CS)
     cols = panel.shape[1] // CS
     steps = cols // WIDTH
     return pl.pallas_call(
-        project_kernel,
-        in_specs=[IN_SMEM] + [IN_PLACE] * 6,
-        out_specs=IN_PLACE,
-        out_shape=jax.ShapeDtypeStruct((cols, rank), F32),
+        chip_kernel,
+        in_specs=[IN_SMEM] * 2 + [IN_VMEM] * 2 + [IN_PLACE] * 2,
+        out_specs=(IN_VMEM, IN_PLACE),
+        out_shape=(
+            jax.ShapeDtypeStruct((ZS * XS, share // (ZS * XS), rank), F32),
+            jax.ShapeDtypeStruct((cols, rank), F32),
+        ),
         scratch_shapes=[
-            pltpu.VMEM((4, rows, rank), BF16),
+            pltpu.VMEM((2 * CS, rows, rank), BF16),
+            pltpu.VMEM((CS * share, rows), F32),
+            pltpu.VMEM((share, rank), F32),
             pltpu.VMEM((steps, rows, WIDTH), F32),
             pltpu.VMEM((steps, rows, WIDTH), F32),
             pltpu.VMEM((steps, WIDTH, rank), F32),
-            pltpu.SemaphoreType.DMA((4,)),
             pltpu.SemaphoreType.DMA((steps,)),
             pltpu.SemaphoreType.DMA((steps,)),
             pltpu.SemaphoreType.DMA((steps,)),
         ],
         compiler_params=params(57),
         cost_estimate=cost(12 * rank * rows * cols, 12 * cols * (rows + rank)),
-        name="project_product",
-    )(core, *sketches, panel, arrived)
+        name="chip_products",
+    )(y, core, own, other, panel, arrived)
 
 
 def exact_dot(left, right, dims):
@@ -325,9 +290,14 @@
     scales = []
     for s in range(count):
         first, u = divmod(s, 8)
-        pivot = spread(columns[s][first], u)
+        if s == 0:
+            pivot = spread(columns[0][0], 0)
         scales.append(lax.rsqrt(pivot))
         inverse = 1.0 / pivot
+        if s + 1 < count:
+            after, at = divmod(s + 1, 8)
+            beside = spread(columns[s][after], at)
+            pivot = spread(columns[s + 1][after], at) - (beside * inverse) * beside
         factor = {v: columns[s][v] * inverse for v in range(first, tiles)}
         factor[first] = jnp.where(sub > u, factor[first], 0.0)
         for t in range(s + 1, count):
@@ -353,7 +323,7 @@
     rank = gram_ref.shape[1]
     low = BLOCK * d
     here = slice(low, low + BLOCK)
-    right = gram_ref[:, low:]
+    right = gram_ref[here, low:]
     left = None
     for k in range(d):
         column = upper[k][:, here]
@@ -386,12 +356,10 @@
 def factor_step(d, gram, upper, inverse):
     rank = gram.shape[1]
     out = jax.ShapeDtypeStruct((BLOCK, rank), F32)
-    first = pl.BlockSpec((BLOCK, rank), lambda i: (0, 0))
     return pl.pallas_call(
         functools.partial(factor_kernel, d),
-        grid=(1,),
-        in_specs=[pl.BlockSpec((BLOCK, rank), lambda i: (d, 0))] + [first] * (2 * d),
-        out_specs=(first, first),
+        in_specs=[IN_VMEM] * (1 + 2 * d),
+        out_specs=(IN_VMEM, IN_VMEM),
         out_shape=(out, out),
         scratch_shapes=[pltpu.VMEM((BLOCK, 2 * BLOCK), F32)],
         compiler_params=params(24),
@@ -406,7 +374,47 @@
         up, inv = factor_step(d, gram, upper, inverse)
         upper.append(up)
         inverse.append(inv)
-    return jnp.concatenate(upper, 0), jnp.concatenate(inverse, 0)
+    return jnp.concatenate(upper, 0), inverse
+
+
+def apply_kernel(scale, core_ref, total_ref, *refs):
+    inverse, (kept_ref, away_ref, total, result, sem) = refs[:-5], refs[-5:]
+    load = pltpu.make_async_copy(total_ref, total, sem)
+    load.start()
+    load.wait()
+    high, low = split(total[...])
+    across = lambda a, b: lax.dot_general(a, b, (((1,), (1,)), ((), ())), preferred_element_type=F32)
+    for d, rows_ref in enumerate(inverse):
+        end = BLOCK * (d + 1)
+        rows_high, rows_low = split(rows_ref[:, :end])
+        term = across(rows_high, high[:, :end])
+        term += across(rows_high, low[:, :end]) + across(rows_low, high[:, :end])
+        result[BLOCK * d : end, :] = term * scale
+    count, share, _ = kept_ref.shape
+    core = core_ref[0]
+    for k in range(count):
+        at = lambda part: pl.ds(pl.multiple_of((CS * k + part) * share, share), share)
+        kept_ref[k] = result[at(core), :]
+        away_ref[k] = result[at(1 - core), :]
+
+
+def apply_inverse(core, inverse, total, scale):
+    cols, rank = total.shape
+    out = jax.ShapeDtypeStruct((ZS * XS, rank // (ZS * XS * CS), cols), F32)
+    return pl.pallas_call(
+        functools.partial(apply_kernel, scale),
+        in_specs=[IN_SMEM, IN_PLACE] + [IN_VMEM] * len(inverse),
+        out_specs=(IN_VMEM, IN_VMEM),
+        out_shape=(out, out),
+        scratch_shapes=[
+            pltpu.VMEM((cols, rank), F32),
+            pltpu.VMEM((rank, cols), F32),
+            pltpu.SemaphoreType.DMA,
+        ],
+        compiler_params=params(24),
+        cost_estimate=cost(6 * rank * rank * cols, 8 * rank * (rank + cols)),
+        name="apply_inverse",
+    )(core, total, *inverse)
 
 
 def shards(panel, sketch_matrix):
@@ -421,23 +429,35 @@
 
     with jax.named_scope("sketch"):
         arrived = swap_core(panel)
-        pieces = sketch_product(y, panel, sketch_matrix)
-        own = place_blocks(y, ring_gather_y(ring_sum_y(*pieces)))
+        block = local_rows // YS
+        half = block // 2
+        far = sketch_product(
+            y,
+            panel,
+            sketch_matrix,
+            ((2, 0, half), (1, half, half), (3, 0, half), (2, half, half)),
+            (block, block),
+        )
+        far, panel = lax.optimization_barrier((far, panel))
+        near = sketch_product(
+            y,
+            panel,
+            sketch_matrix,
+            ((1, 0, half), (3, half, half), (0, 0, block)),
+            (half, half, block),
+        )
+        own = place_blocks(y, ring_gather_y(ring_sum_y(*far, *near)))
         other = swap_core(own)
 
-    with jax.named_scope("gram"):
-        gram, *sketches = gram_product(y, core, own, other)
-        gram, *sketches = together(gram, *sketches)
-        gram = exchange(gram.reshape(ZS * XS, -1, rank), ZX_GROUPS)
-
     with jax.named_scope("project"):
-        total = project_product(core, sketches, panel, arrived)
+        gram, total = chip_products(y, core, own, other, panel, arrived)
         total = lax.psum_scatter(
             total, "row", scatter_dimension=0, axis_index_groups=Z_GROUPS, tiled=True
         )
 
     with jax.named_scope("gram"):
-        gram = exchange(repeat(gram.sum(0), ZS * XS), ZX_GROUPS).reshape(-1, rank)
+        gram = exchange(gram, ZX_GROUPS).sum(0)
+        gram = exchange(repeat(gram, ZS * XS), ZX_GROUPS).reshape(-1, rank)
         gram = place_blocks(y, ring_gather_y(gram)).reshape(YS, -1, rank)
         gram = place({0: gram, 1: swap_core(gram)}, CS, c)
         gram = gram.transpose(1, 0, 2, 3).reshape(rank, rank)
@@ -446,16 +466,13 @@
         upper, inverse = factorize(gram)
 
     with jax.named_scope("apply"):
-        result = lax.dot_general(
-            inverse,
-            total,
-            (((1,), (1,)), ((), ())),
-            precision=lax.Precision.HIGH,
-            preferred_element_type=F32,
+        kept, away = apply_inverse(core, inverse, total, norm_scale)
+        arrived = swap_core(away)
+        first = c == 0
+        result = jnp.stack(
+            [jnp.where(first, kept, arrived), jnp.where(first, arrived, kept)], axis=1
         )
-        width = result.shape[1]
-        result = exchange(result.reshape(-1, row_share, width), None)
-        result = result.reshape(ZS, XS, CS, row_share, width).sum(1) * norm_scale
+        result = exchange(result, ZX_GROUPS).reshape(ZS, XS, CS, row_share, -1).sum(1)
         projected = result.transpose(2, 1, 0, 3).reshape(row_share, local_cols)
         spread = lax.dynamic_slice_in_dim(upper, row * row_share, row_share, 0) * norm_scale
     return (projected, spread)

time: 177 us -> 174 us (0.983)
  waiting for transfers between devices: 41.8 us -> 35.7 us
  Pallas kernels: 44 us -> 48.8 us
  matrix products: 2.46 us -> 0 us
    ppermute x12, waiting for transfers between devices: 20.9 us -> 14.8 us  [send_y(): return lax.ppermute(array, 'col', [(i, (i + step) % YS) for i in range(YS)])]
    pallas_call x7 -> x8, Pallas kernels: 43.9 us -> 48.7 us  [the longest x4 19.3 us: factor_step(): pl.pallas_call(functools.partial(factor_kernel, d), in_specs=[IN_VMEM] *...]
    dot_general x1 -> x0, matrix products: 2.46 us -> none  [shards(): lax.dot_general(inverse, total, (((1,), (1,)), ((), ())), precision=lax.P...]
    unnamed x9 -> x7, local copies, waits for them, and re-layouts: 3.99 us -> 2.75 us
    ppermute x3 -> x4, waiting for transfers between devices: 3.65 us -> 4.81 us  [swap_core(): return lax.ppermute(array, 'row', row_pairs(lambda z, x, c: (z, x, 1 - c)))]
    ppermute x3 -> x4, starting transfers between devices: 12.4 us -> 12.4 us  [swap_core(): return lax.ppermute(array, 'row', row_pairs(lambda z, x, c: (z, x, 1 - c)))]
  transfers between devices with their start and end apart: 17 -> 18, of which waited for: 9 -> 9; matrix products, arithmetic and copies ran while one was open for 2% -> 2% of each run, Pallas kernels for 18% -> 21%
where the time goes in v2:
time: 174 us; the launch traced here: 173 us
  Pallas kernels  48.8 us (28%)
  waiting for transfers between devices  35.7 us (21%)
  blocking collectives  33.6 us (19%)
  starting transfers between devices  33.4 us (19%)
  between operations  14.3 us (8%)
  local copies, waits for them, and re-layouts  4.07 us (2%)
  other arithmetic  2.84 us (2%)
    all_to_all x2, blocking collectives, exchange(): return lax.all_to_all(array, 'row', 0, 0, axis_index_groups=groups)  33.6 us
    pallas_call x4, Pallas kernels, factor_step(): pl.pallas_call(functools.partial(factor_kernel, d), in_specs=[IN_VMEM] *...  19.3 us
    ppermute x12, starting transfers between devices, send_y(): return lax.ppermute(array, 'col', [(i, (i + step) % YS) for i in range(YS)])  17.1 us
    pallas_call x2, Pallas kernels, sketch_product(): pl.pallas_call(functools.partial(sketch_kernel, pieces), in_specs=[IN_SME...  16.4 us
    all_to_all x1, waiting for transfers between devices, exchange(): return lax.all_to_all(array, 'row', 0, 0, axis_index_groups=groups)  16 us
    ppermute x12, waiting for transfers between devices, send_y(): return lax.ppermute(array, 'col', [(i, (i + step) % YS) for i in range(YS)])  14.8 us
    ppermute x4, starting transfers between devices, swap_core(): return lax.ppermute(array, 'row', row_pairs(lambda z, x, c: (z, x, 1 - c)))  12.4 us
    pallas_call x1, Pallas kernels, chip_products(): pl.pallas_call(chip_kernel, in_specs=[IN_SMEM] * 2 + [IN_VMEM] * 2 + [IN_...  12.2 us
  transfers between devices with their start and end apart: 18, of which 9 were waited for; matrix products, arithmetic and copies ran while one was open for 2% of the time, Pallas kernels for 21%

profile of v2, /device:TPU:1, one launch (start us, length us, event | category | flops | bytes accessed | tf_op | source)
XLA Modules:
  0.0 172.7 jit_solution(8643030134292373482)
XLA Ops:
  7.2 3.3 %collective-permute-start.9 = (f32[512,4096]{1,0:T(8,128)}, f32[512,4096]{1,0:T(8,128)}, u32[]{:S(2)}, u32[]{:S(2)}) collective-permute-start(f32[512,4096]{1,0:T(8,128)} %panel_ref.3), channel_id=1, source_target_pairs={{0,4},{4,0},{8,12},{12,8},{16,20},{20,16},{24,28},{28,24},{32,36},... | collective-permute-start | bytes 25165832 | tf_op jit(solution)/shard_map/sketch/ppermute | solution.py:40
  10.5 8.3 %sketch_product.2 = (f32[128,512]{1,0:T(8,128)}, f32[128,512]{1,0:T(8,128)}) custom-call(s32[1]{0:T(128)} %bitcast.1.y_ref, f32[512,4096]{1,0:T(8,128)} %panel_ref.3, f32[4096,512]{1,0:T(8,128)} %matrix_ref.3), custom_call_target="tpu_custom_call" | custom-call | flops 3221225472 | bytes 12582912 | tf_op jit(solution)/shard_map/sketch/sketch_product/pallas_call | solution.py:148
  19.0 2.7 %collective-permute-start.1 = (f32[128,512]{1,0:T(8,128)}, f32[128,512]{1,0:T(8,128)S(1)}, u32[]{:S(2)}, u32[]{:S(2)}) collective-permute-start(f32[128,512]{1,0:T(8,128)} %get-tuple-element.37), channel_id=1, source_target_pairs={{0,3},{1,0},{2,1},{3,2},{4,7},{5,4},{6,5},{7,6},{8,11},{9,8},{10,9... | collective-permute-start | bytes 786440 | tf_op jit(solution)/shard_map/sketch/ppermute | solution.py:36
  21.6 8.1 %sketch_product.3 = (f32[64,512]{1,0:T(8,128)}, f32[64,512]{1,0:T(8,128)}, f32[128,512]{1,0:T(8,128)}) custom-call(s32[1]{0:T(128)} %bitcast.1.y_ref, f32[512,4096]{1,0:T(8,128)} %panel_ref.3, f32[4096,512]{1,0:T(8,128)} %matrix_ref.3), custom_call_target="tpu_custom_call" | custom-call | flops 3221225472 | bytes 12582912 | tf_op jit(solution)/shard_map/sketch/sketch_product/pallas_call | solution.py:148
  30.9 2.7 %collective-permute-start.3 = (f32[64,512]{1,0:T(8,128)S(1)}, f32[64,512]{1,0:T(8,128)S(1)}, u32[]{:S(2)}, u32[]{:S(2)}) collective-permute-start(f32[64,512]{1,0:T(8,128)S(1)} %get-tuple-element.43), channel_id=1, source_target_pairs={{0,3},{1,0},{2,1},{3,2},{4,7},{5,4},{6,5},{7,6},{8,11},{9,8},{10,9... | collective-permute-start | bytes 393224 | tf_op jit(solution)/shard_map/sketch/ppermute | solution.py:36
  33.5 3.0 %collective-permute-done.2 = f32[64,512]{1,0:T(8,128)S(1)} collective-permute-done((f32[64,512]{1,0:T(8,128)S(1)}, f32[64,512]{1,0:T(8,128)S(1)}, u32[]{:S(2)}, u32[]{:S(2)}) %collective-permute-start.2) | collective-permute-done | bytes 131104 | tf_op jit(solution)/shard_map/sketch/ppermute | solution.py:36
  37.7 2.7 %collective-permute-start.5 = (f32[128,512]{1,0:T(8,128)S(1)}, f32[128,512]{1,0:T(8,128)S(1)}, u32[]{:S(2)}, u32[]{:S(2)}) collective-permute-start(f32[128,512]{1,0:T(8,128)S(1)} %maximum_add_fusion.own), channel_id=1, source_target_pairs={{0,3},{1,0},{2,1},{3,2},{4,7},{5,4},{6,5},{7,6},{8,11},{9,8},{10,9... | collective-permute-start | bytes 786440 | tf_op jit(solution)/shard_map/sketch/ppermute | solution.py:36
  40.3 4.9 %collective-permute-done.4.before = f32[128,512]{1,0:T(8,128)S(1)} collective-permute-done((f32[128,512]{1,0:T(8,128)S(1)}, f32[128,512]{1,0:T(8,128)S(1)}, u32[]{:S(2)}, u32[]{:S(2)}) %collective-permute-start.4) | collective-permute-done | bytes 262176 | tf_op jit(solution)/shard_map/sketch/ppermute | solution.py:36
  45.5 2.5 %collective-permute-start.7 = (f32[64,512]{1,0:T(8,128)S(1)}, f32[64,512]{1,0:T(8,128)S(1)}, u32[]{:S(2)}, u32[]{:S(2)}) collective-permute-start(f32[64,512]{1,0:T(8,128)S(1)} %slice.29), channel_id=1, source_target_pairs={{0,3},{1,0},{2,1},{3,2},{4,7},{5,4},{6,5},{7,6},{8,11},{9,8},{10,9... | collective-permute-start | bytes 393224 | tf_op jit(solution)/shard_map/sketch/ppermute | solution.py:36
  48.1 2.3 %collective-permute-done.6.head = f32[64,512]{1,0:T(8,128)S(1)} collective-permute-done((f32[64,512]{1,0:T(8,128)S(1)}, f32[64,512]{1,0:T(8,128)S(1)}, u32[]{:S(2)}, u32[]{:S(2)}) %collective-permute-start.6) | collective-permute-done | bytes 131104 | tf_op jit(solution)/shard_map/sketch/ppermute | solution.py:36
  50.4 3.6 %collective-permute-start.8 = (f32[512,512]{1,0:T(8,128)S(1)}, f32[512,512]{1,0:T(8,128)S(1)}, u32[]{:S(2)}, u32[]{:S(2)}) collective-permute-start(f32[512,512]{1,0:T(8,128)S(1)} %bitcast.26), channel_id=1, source_target_pairs={{0,4},{4,0},{8,12},{12,8},{16,20},{20,16},{24,28},{28,24},{32,36},... | collective-permute-start | bytes 3145736 | tf_op jit(solution)/shard_map/sketch/ppermute | solution.py:40
  54.0 2.3 %collective-permute-done.8.other_ref = f32[512,512]{1,0:T(8,128)S(1)} collective-permute-done((f32[512,512]{1,0:T(8,128)S(1)}, f32[512,512]{1,0:T(8,128)S(1)}, u32[]{:S(2)}, u32[]{:S(2)}) %collective-permute-start.8) | collective-permute-done | bytes 1048608 | tf_op jit(solution)/shard_map/sketch/ppermute | solution.py:40
  57.3 12.2 %chip_products.1 = (f32[32,2,512]{2,1,0:T(2,128)}, f32[2048,512]{1,0:T(8,128)}) custom-call(s32[1]{0:T(128)} %bitcast.1.y_ref, s32[1]{0:T(128)} %bitcast.core_ref, f32[512,512]{1,0:T(8,128)} %bitcast.27, f32[512,512]{1,0:T(8,128)} %copy-done.2, f32[512,4096]{1,0:T(8,128)} %panel_ref.3, f32[512,4096]{1,0:T(8,128)} %collective-permute-done.9.arrived_ref), custom_call_target="tpu_custom_call" | custom-call | flops 6442450944 | bytes 25165824 | tf_op jit(solution)/shard_map/project/chip_products/pallas_call | solution.py:247
  69.5 19.0 %all_to_all.15 = f32[32,2,512]{2,1,0:T(2,128)S(1)} all-to-all(f32[32,2,512]{2,1,0:T(2,128)} %get-tuple-element.49), channel_id=1, replica_groups={{0,8,16,24,32,40,48,56,64,72,80,88,96,104,112,120,128,136,144,152,160,1..., dimensions={0} | all-to-all | bytes 262144 | tf_op jit(solution)/shard_map/gram/all_to_all | solution.py:44
  88.6 14.7 %all_to_all.16 = f32[32,2,512]{2,1,0:T(2,128)S(1)} all-to-all(f32[32,2,512]{2,1,0:T(2,128)S(1)} %broadcast_in_dim.17), channel_id=1, replica_groups={{0,8,16,24,32,40,48,56,64,72,80,88,96,104,112,120,128,136,144,152,160,1..., dimensions={0} | all-to-all | bytes 262144 | tf_op jit(solution)/shard_map/gram/all_to_all | solution.py:44
  106.5 2.7 %collective-permute-done.10.before = f32[64,512]{1,0:T(8,128)S(1)} collective-permute-done((f32[64,512]{1,0:T(8,128)S(1)}, f32[64,512]{1,0:T(8,128)S(1)}, u32[]{:S(2)}, u32[]{:S(2)}) %collective-permute-start.10) | collective-permute-done | bytes 131104 | tf_op jit(solution)/shard_map/gram/ppermute | solution.py:36
  112.1 2.0 %collective-permute-done.12.head = f32[32,512]{1,0:T(8,128)S(1)} collective-permute-done((f32[32,512]{1,0:T(8,128)S(1)}, f32[32,512]{1,0:T(8,128)S(1)}, u32[]{:S(2)}, u32[]{:S(2)}) %collective-permute-start.12) | collective-permute-done | bytes 65568 | tf_op jit(solution)/shard_map/gram/ppermute | solution.py:36
  114.1 5.0 %collective-permute-start.14 = (f32[4,64,512]{2,1,0:T(8,128)S(1)}, f32[4,64,512]{2,1,0:T(8,128)S(1)}, u32[]{:S(2)}, u32[]{:S(2)}) collective-permute-start(f32[4,64,512]{2,1,0:T(8,128)S(1)} %place_blocks.3), channel_id=1, source_target_pairs={{0,4},{4,0},{8,12},{12,8},{16,20},{20,16},{24,28},{28,24},{32,36},... | collective-permute-start | bytes 1572872 | tf_op jit(solution)/shard_map/gram/ppermute | solution.py:40
  120.7 4.4 %factor_step.4 = (f32[128,512]{1,0:T(8,128)S(1)}, f32[128,512]{1,0:T(8,128)S(1)}) custom-call(f32[512,512]{1,0:T(8,128)S(1)} %bitcast.28), custom_call_target="tpu_custom_call" | custom-call | flops 5000000000 | bytes 786432 | tf_op jit(solution)/shard_map/factor/factor_step/pallas_call | solution.py:359
  125.1 4.7 %factor_step.5 = (f32[128,512]{1,0:T(8,128)S(1)}, f32[128,512]{1,0:T(8,128)S(1)}) custom-call(f32[512,512]{1,0:T(8,128)S(1)} %bitcast.29, f32[128,512]{1,0:T(8,128)S(1)} %get-tuple-element.53.refs_1_, f32[128,512]{1,0:T(8,128)S(1)} %get-tuple-element.52.refs_2_.refs_3_.refs_4_.refs_0_), custom_call_target="tpu_custom_call" | custom-call | flops 5000000000 | bytes 1310720 | tf_op jit(solution)/shard_map/factor/factor_step/pallas_call | solution.py:359
  129.8 4.9 %factor_step.6 = (f32[128,512]{1,0:T(8,128)S(1)}, f32[128,512]{1,0:T(8,128)S(1)}) custom-call(f32[512,512]{1,0:T(8,128)S(1)} %bitcast.30, f32[128,512]{1,0:T(8,128)S(1)} %get-tuple-element.53.refs_1_, f32[128,512]{1,0:T(8,128)S(1)} %get-tuple-element.55.refs_2_, f32[128,512]{1,0:T(8,128)S(1)} %get-tuple-element.52.refs_2_.refs_3_.refs_4_.refs_0_, ...), custom_call_target="tpu_custom_call" | custom-call | flops 5000000000 | bytes 1835008 | tf_op jit(solution)/shard_map/factor/factor_step/pallas_call | solution.py:359
  134.7 5.3 %factor_step.7 = (f32[128,512]{1,0:T(8,128)S(1)}, f32[128,512]{1,0:T(8,128)S(1)}) custom-call(f32[512,512]{1,0:T(8,128)S(1)} %bitcast.31, f32[128,512]{1,0:T(8,128)S(1)} %get-tuple-element.53.refs_1_, f32[128,512]{1,0:T(8,128)S(1)} %get-tuple-element.55.refs_2_, f32[128,512]{1,0:T(8,128)S(1)} %get-tuple-element.57.refs_3_, ...), custom_call_target="tpu_custom_call" | custom-call | flops 5000000000 | bytes 2359296 | tf_op jit(solution)/shard_map/factor/factor_step/pallas_call | solution.py:359
  144.4 3.9 %all-to-all-start.2 = ((f32[32,2,8,256]{3,2,1,0:T(8,128)}), f32[32,2,8,256]{3,2,1,0:T(8,128)S(1)}, u32[]{:S(2)}, u32[]{:S(2)}) async-start(f32[32,2,8,256]{3,2,1,0:T(8,128)} %copy.14), calls=%async_computation.3 | async-start | bytes 1048576 | tf_op jit(solution)/shard_map/apply/all_to_all | solution.py:44
  149.0 16.0 %all-to-all-done.2 = f32[32,2,8,256]{3,2,1,0:T(8,128)S(1)} async-done(((f32[32,2,8,256]{3,2,1,0:T(8,128)}), f32[32,2,8,256]{3,2,1,0:T(8,128)S(1)}, u32[]{:S(2)}, u32[]{:S(2)}) %all-to-all-start.2) | async-done | bytes 524320 | tf_op jit(solution)/shard_map/apply/all_to_all | solution.py:44
  (52 shorter events, 17.5 us)
Async XLA Ops:
  7.2 132.8 %reduce-scatter.2.cloned.1.call-start = ((), (), s32[]{:S(2)}) async-start(), calls=%async_computation.4 | async-start | bytes 4718592 | tf_op jit(solution)/shard_map/project/reduce_scatter | solution.py:454
  7.2 49.1 %collective-permute-start.9 = (f32[512,4096]{1,0:T(8,128)}, f32[512,4096]{1,0:T(8,128)}, u32[]{:S(2)}, u32[]{:S(2)}) collective-permute-start(f32[512,4096]{1,0:T(8,128)} %panel_ref.3), channel_id=1, source_target_pairs={{0,4},{4,0},{8,12},{12,8},{16,20},{20,16},{24,28},{28,24},{32,36},... | collective-permute-start | bytes 25165832 | tf_op jit(solution)/shard_map/sketch/ppermute | solution.py:40
  18.9 10.8 %collective-permute-start = (f32[128,512]{1,0:T(8,128)}, f32[128,512]{1,0:T(8,128)S(1)}, u32[]{:S(2)}, u32[]{:S(2)}) collective-permute-start(f32[128,512]{1,0:T(8,128)} %get-tuple-element.36), channel_id=1, source_target_pairs={{0,1},{1,2},{2,3},{3,0},{4,5},{5,6},{6,7},{7,4},{8,9},{9,10},{10,1... | collective-permute-start | bytes 786440 | tf_op jit(solution)/shard_map/sketch/ppermute | solution.py:36
  19.0 10.8 %collective-permute-start.1 = (f32[128,512]{1,0:T(8,128)}, f32[128,512]{1,0:T(8,128)S(1)}, u32[]{:S(2)}, u32[]{:S(2)}) collective-permute-start(f32[128,512]{1,0:T(8,128)} %get-tuple-element.37), channel_id=1, source_target_pairs={{0,3},{1,0},{2,1},{3,2},{4,7},{5,4},{6,5},{7,6},{8,11},{9,8},{10,9... | collective-permute-start | bytes 786440 | tf_op jit(solution)/shard_map/sketch/ppermute | solution.py:36
  30.8 5.8 %collective-permute-start.2 = (f32[64,512]{1,0:T(8,128)S(1)}, f32[64,512]{1,0:T(8,128)S(1)}, u32[]{:S(2)}, u32[]{:S(2)}) collective-permute-start(f32[64,512]{1,0:T(8,128)S(1)} %get-tuple-element.42), channel_id=1, source_target_pairs={{0,1},{1,2},{2,3},{3,0},{4,5},{5,6},{6,7},{7,4},{8,9},{9,10},{10,1... | collective-permute-start | bytes 393224 | tf_op jit(solution)/shard_map/sketch/ppermute | solution.py:36
  30.9 5.7 %collective-permute-start.3 = (f32[64,512]{1,0:T(8,128)S(1)}, f32[64,512]{1,0:T(8,128)S(1)}, u32[]{:S(2)}, u32[]{:S(2)}) collective-permute-start(f32[64,512]{1,0:T(8,128)S(1)} %get-tuple-element.43), channel_id=1, source_target_pairs={{0,3},{1,0},{2,1},{3,2},{4,7},{5,4},{6,5},{7,6},{8,11},{9,8},{10,9... | collective-permute-start | bytes 393224 | tf_op jit(solution)/shard_map/sketch/ppermute | solution.py:36
  37.6 7.6 %collective-permute-start.4 = (f32[128,512]{1,0:T(8,128)S(1)}, f32[128,512]{1,0:T(8,128)S(1)}, u32[]{:S(2)}, u32[]{:S(2)}) collective-permute-start(f32[128,512]{1,0:T(8,128)S(1)} %maximum_add_fusion.own), channel_id=1, source_target_pairs={{0,1},{1,2},{2,3},{3,0},{4,5},{5,6},{6,7},{7,4},{8,9},{9,10},{10,1... | collective-permute-start | bytes 786440 | tf_op jit(solution)/shard_map/sketch/ppermute | solution.py:36
  37.7 7.6 %collective-permute-start.5 = (f32[128,512]{1,0:T(8,128)S(1)}, f32[128,512]{1,0:T(8,128)S(1)}, u32[]{:S(2)}, u32[]{:S(2)}) collective-permute-start(f32[128,512]{1,0:T(8,128)S(1)} %maximum_add_fusion.own), channel_id=1, source_target_pairs={{0,3},{1,0},{2,1},{3,2},{4,7},{5,4},{6,5},{7,6},{8,11},{9,8},{10,9... | collective-permute-start | bytes 786440 | tf_op jit(solution)/shard_map/sketch/ppermute | solution.py:36
  45.2 5.1 %collective-permute-start.6 = (f32[64,512]{1,0:T(8,128)S(1)}, f32[64,512]{1,0:T(8,128)S(1)}, u32[]{:S(2)}, u32[]{:S(2)}) collective-permute-start(f32[64,512]{1,0:T(8,128)S(1)} %slice.28), channel_id=1, source_target_pairs={{0,1},{1,2},{2,3},{3,0},{4,5},{5,6},{6,7},{7,4},{8,9},{9,10},{10,1... | collective-permute-start | bytes 393224 | tf_op jit(solution)/shard_map/sketch/ppermute | solution.py:36
  45.5 4.8 %collective-permute-start.7 = (f32[64,512]{1,0:T(8,128)S(1)}, f32[64,512]{1,0:T(8,128)S(1)}, u32[]{:S(2)}, u32[]{:S(2)}) collective-permute-start(f32[64,512]{1,0:T(8,128)S(1)} %slice.29), channel_id=1, source_target_pairs={{0,3},{1,0},{2,1},{3,2},{4,7},{5,4},{6,5},{7,6},{8,11},{9,8},{10,9... | collective-permute-start | bytes 393224 | tf_op jit(solution)/shard_map/sketch/ppermute | solution.py:36
  50.4 5.9 %copy-start = (f32[4,128,512]{2,1,0:T(8,128)}, f32[4,128,512]{2,1,0:T(8,128)S(1)}, u32[]{:S(2)}) copy-start(f32[4,128,512]{2,1,0:T(8,128)S(1)} %place_blocks.2) | copy-start | bytes 3145732
  50.4 5.9 %collective-permute-start.8 = (f32[512,512]{1,0:T(8,128)S(1)}, f32[512,512]{1,0:T(8,128)S(1)}, u32[]{:S(2)}, u32[]{:S(2)}) collective-permute-start(f32[512,512]{1,0:T(8,128)S(1)} %bitcast.26), channel_id=1, source_target_pairs={{0,4},{4,0},{8,12},{12,8},{16,20},{20,16},{24,28},{28,24},{32,36},... | collective-permute-start | bytes 3145736 | tf_op jit(solution)/shard_map/sketch/ppermute | solution.py:40
  56.3 1.0 copy-start.2
  103.4 5.8 %collective-permute-start.10 = (f32[64,512]{1,0:T(8,128)S(1)}, f32[64,512]{1,0:T(8,128)S(1)}, u32[]{:S(2)}, u32[]{:S(2)}) collective-permute-start(f32[64,512]{1,0:T(8,128)S(1)} %reshape.29.own), channel_id=1, source_target_pairs={{0,1},{1,2},{2,3},{3,0},{4,5},{5,6},{6,7},{7,4},{8,9},{9,10},{10,1... | collective-permute-start | bytes 393224 | tf_op jit(solution)/shard_map/gram/ppermute | solution.py:36
  104.6 4.6 %collective-permute-start.11 = (f32[64,512]{1,0:T(8,128)S(1)}, f32[64,512]{1,0:T(8,128)S(1)}, u32[]{:S(2)}, u32[]{:S(2)}) collective-permute-start(f32[64,512]{1,0:T(8,128)S(1)} %reshape.29.own), channel_id=1, source_target_pairs={{0,3},{1,0},{2,1},{3,2},{4,7},{5,4},{6,5},{7,6},{8,11},{9,8},{10,9... | collective-permute-start | bytes 393224 | tf_op jit(solution)/shard_map/gram/ppermute | solution.py:36
  109.2 4.8 %collective-permute-start.12 = (f32[32,512]{1,0:T(8,128)S(1)}, f32[32,512]{1,0:T(8,128)S(1)}, u32[]{:S(2)}, u32[]{:S(2)}) collective-permute-start(f32[32,512]{1,0:T(8,128)S(1)} %slice.30), channel_id=1, source_target_pairs={{0,1},{1,2},{2,3},{3,0},{4,5},{5,6},{6,7},{7,4},{8,9},{9,10},{10,1... | collective-permute-start | bytes 196616 | tf_op jit(solution)/shard_map/gram/ppermute | solution.py:36
  110.3 3.7 %collective-permute-start.13 = (f32[32,512]{1,0:T(8,128)S(1)}, f32[32,512]{1,0:T(8,128)S(1)}, u32[]{:S(2)}, u32[]{:S(2)}) collective-permute-start(f32[32,512]{1,0:T(8,128)S(1)} %slice.31), channel_id=1, source_target_pairs={{0,3},{1,0},{2,1},{3,2},{4,7},{5,4},{6,5},{7,6},{8,11},{9,8},{10,9... | collective-permute-start | bytes 196616 | tf_op jit(solution)/shard_map/gram/ppermute | solution.py:36
  114.1 6.5 %collective-permute-start.14 = (f32[4,64,512]{2,1,0:T(8,128)S(1)}, f32[4,64,512]{2,1,0:T(8,128)S(1)}, u32[]{:S(2)}, u32[]{:S(2)}) collective-permute-start(f32[4,64,512]{2,1,0:T(8,128)S(1)} %place_blocks.3), channel_id=1, source_target_pairs={{0,4},{4,0},{8,12},{12,8},{16,20},{20,16},{24,28},{28,24},{32,36},... | collective-permute-start | bytes 1572872 | tf_op jit(solution)/shard_map/gram/ppermute | solution.py:40
  140.0 1.0 copy-start.1
  141.8 1.6 collective-permute-start.15
  144.4 20.6 %all-to-all-start.2 = ((f32[32,2,8,256]{3,2,1,0:T(8,128)}), f32[32,2,8,256]{3,2,1,0:T(8,128)S(1)}, u32[]{:S(2)}, u32[]{:S(2)}) async-start(f32[32,2,8,256]{3,2,1,0:T(8,128)} %copy.14), calls=%async_computation.3 | async-start | bytes 1048576 | tf_op jit(solution)/shard_map/apply/all_to_all | solution.py:44
Sparse Core Ops, SparseCore 0:
  69.7 59.9 reduce-scatter.1

commit v3 on v2

--- a/solution.py
+++ b/solution.py
@@ -10,7 +10,7 @@
 
 ZS, XS, CS, YS = 8, 4, 2, 4
 BLOCK = 128
-PIVOTS = 32
+PIVOTS = 16
 WIDTH = 512
 F32, BF16 = jnp.float32, jnp.bfloat16
 
@@ -269,10 +269,12 @@
     )(y, core, own, other, panel, arrived)
 
 
-def exact_dot(left, right, dims):
-    return lax.dot_general(
-        left, right, (dims, ((), ())), precision=lax.Precision.HIGHEST, preferred_element_type=F32
+def block_dot(left, right, dims):
+    left, right = split(left), split(right)
+    term = lambda i, j: lax.dot_general(
+        left[i], right[j], (dims, ((), ())), preferred_element_type=F32
     )
+    return term(0, 0) + term(0, 1) + term(1, 0)
 
 
 def eliminate(rows, base):
@@ -327,8 +329,8 @@
     left = None
     for k in range(d):
         column = upper[k][:, here]
-        right = right - exact_dot(column, upper[k][:, low:], ((0,), (0,)))
-        term = exact_dot(column, inverse[k][:, :low], ((0,), (0,)))
+        right = right - block_dot(column, upper[k][:, low:], ((0,), (0,)))
+        term = block_dot(column, inverse[k][:, :low], ((0,), (0,)))
         left = -term if left is None else left - term
     row_ids = lax.broadcasted_iota(jnp.int32, (BLOCK, BLOCK), 0)
     column_ids = lax.broadcasted_iota(jnp.int32, (BLOCK, BLOCK), 1)
@@ -337,7 +339,7 @@
     for p in range(0, BLOCK, PIVOTS):
         rows = work[p : p + PIVOTS, :]
         if p:
-            rows = rows - exact_dot(work[:p, p : p + PIVOTS], work[:p, :], ((0,), (0,)))
+            rows = rows - block_dot(work[:p, p : p + PIVOTS], work[:p, :], ((0,), (0,)))
         tiles = [rows[v : v + 8] for v in range(0, PIVOTS, 8)]
         for v, parts in enumerate(eliminate(tiles, p)):
             for q, part in enumerate(parts):
@@ -348,9 +350,9 @@
     upper_ref[:, here] = jnp.where(row_ids <= column_ids, work[:, :BLOCK], 0.0)
     inverse_ref[:, here] = block_inverse
     if low + BLOCK < rank:
-        upper_ref[:, low + BLOCK :] = exact_dot(block_inverse, right[:, BLOCK:], ((1,), (0,)))
+        upper_ref[:, low + BLOCK :] = block_dot(block_inverse, right[:, BLOCK:], ((1,), (0,)))
     if d:
-        inverse_ref[:, :low] = exact_dot(block_inverse, left, ((1,), (0,)))
+        inverse_ref[:, :low] = block_dot(block_inverse, left, ((1,), (0,)))
 
 
 def factor_step(d, gram, upper, inverse):
@@ -377,8 +379,8 @@
     return jnp.concatenate(upper, 0), inverse
 
 
-def apply_kernel(scale, core_ref, total_ref, *refs):
-    inverse, (kept_ref, away_ref, total, result, sem) = refs[:-5], refs[-5:]
+def apply_kernel(scale, total_ref, *refs):
+    inverse, (out_ref, total, sem) = refs[:-3], refs[-3:]
     load = pltpu.make_async_copy(total_ref, total, sem)
     load.start()
     load.wait()
@@ -389,32 +391,21 @@
         rows_high, rows_low = split(rows_ref[:, :end])
         term = across(rows_high, high[:, :end])
         term += across(rows_high, low[:, :end]) + across(rows_low, high[:, :end])
-        result[BLOCK * d : end, :] = term * scale
-    count, share, _ = kept_ref.shape
-    core = core_ref[0]
-    for k in range(count):
-        at = lambda part: pl.ds(pl.multiple_of((CS * k + part) * share, share), share)
-        kept_ref[k] = result[at(core), :]
-        away_ref[k] = result[at(1 - core), :]
-
-
-def apply_inverse(core, inverse, total, scale):
+        out_ref[BLOCK * d : end, :] = term * scale
+
+
+def apply_inverse(inverse, total, scale):
     cols, rank = total.shape
-    out = jax.ShapeDtypeStruct((ZS * XS, rank // (ZS * XS * CS), cols), F32)
     return pl.pallas_call(
         functools.partial(apply_kernel, scale),
-        in_specs=[IN_SMEM, IN_PLACE] + [IN_VMEM] * len(inverse),
-        out_specs=(IN_VMEM, IN_VMEM),
-        out_shape=(out, out),
-        scratch_shapes=[
-            pltpu.VMEM((cols, rank), F32),
-            pltpu.VMEM((rank, cols), F32),
-            pltpu.SemaphoreType.DMA,
-        ],
+        in_specs=[IN_PLACE] + [IN_VMEM] * len(inverse),
+        out_specs=IN_VMEM,
+        out_shape=jax.ShapeDtypeStruct((rank, cols), F32),
+        scratch_shapes=[pltpu.VMEM((cols, rank), F32), pltpu.SemaphoreType.DMA],
         compiler_params=params(24),
         cost_estimate=cost(6 * rank * rank * cols, 8 * rank * (rank + cols)),
         name="apply_inverse",
-    )(core, total, *inverse)
+    )(total, *inverse)
 
 
 def shards(panel, sketch_matrix):
@@ -458,7 +449,7 @@
     with jax.named_scope("gram"):
         gram = exchange(gram, ZX_GROUPS).sum(0)
         gram = exchange(repeat(gram, ZS * XS), ZX_GROUPS).reshape(-1, rank)
-        gram = place_blocks(y, ring_gather_y(gram)).reshape(YS, -1, rank)
+        gram = lax.all_to_all(repeat(gram, YS), "col", 0, 0)
         gram = place({0: gram, 1: swap_core(gram)}, CS, c)
         gram = gram.transpose(1, 0, 2, 3).reshape(rank, rank)
 
@@ -466,13 +457,9 @@
         upper, inverse = factorize(gram)
 
     with jax.named_scope("apply"):
-        kept, away = apply_inverse(core, inverse, total, norm_scale)
-        arrived = swap_core(away)
-        first = c == 0
-        result = jnp.stack(
-            [jnp.where(first, kept, arrived), jnp.where(first, arrived, kept)], axis=1
-        )
-        result = exchange(result, ZX_GROUPS).reshape(ZS, XS, CS, row_share, -1).sum(1)
+        result = apply_inverse(inverse, total, norm_scale)
+        result = exchange(result.reshape(ZS * XS * CS, row_share, -1), None)
+        result = result.reshape(ZS, XS, CS, row_share, -1).sum(1)
         projected = result.transpose(2, 1, 0, 3).reshape(row_share, local_cols)
         spread = lax.dynamic_slice_in_dim(upper, row * row_share, row_share, 0) * norm_scale
     return (projected, spread)

time: 174 us -> 171 us (0.983)
  blocking collectives: 33.6 us -> 44.6 us
  starting transfers between devices: 33.4 us -> 27.3 us
  waiting for transfers between devices: 35.7 us -> 31 us
    all_to_all x0 -> x1, blocking collectives: none -> 11 us  [shards(): gram = lax.all_to_all(repeat(gram, YS), 'col', 0, 0)]
    ppermute x12 -> x8, starting transfers between devices: 17.1 us -> 11.1 us  [send_y(): return lax.ppermute(array, 'col', [(i, (i + step) % YS) for i in range(YS)])]
    ppermute x12 -> x8, waiting for transfers between devices: 14.8 us -> 10.1 us  [send_y(): return lax.ppermute(array, 'col', [(i, (i + step) % YS) for i in range(YS)])]
    pallas_call x4, Pallas kernels: 19.3 us -> 17.3 us  [factor_step(): pl.pallas_call(functools.partial(factor_kernel, d), in_specs=[IN_VMEM] *...]
    ppermute x4 -> x3, waiting for transfers between devices: 4.81 us -> 3.65 us  [swap_core(): return lax.ppermute(array, 'row', row_pairs(lambda z, x, c: (z, x, 1 - c)))]
    ppermute x4 -> x3, starting transfers between devices: 12.4 us -> 11.8 us  [swap_core(): return lax.ppermute(array, 'row', row_pairs(lambda z, x, c: (z, x, 1 - c)))]
  transfers between devices with their start and end apart: 18 -> 13, of which waited for: 9 -> 6; matrix products, arithmetic and copies ran while one was open for 2% -> 2% of each run, Pallas kernels for 21% -> 20%
where the time goes in v3:
time: 171 us
  Pallas kernels  47.6 us (28%)
  blocking collectives  44.6 us (26%)
  waiting for transfers between devices  31 us (18%)
  starting transfers between devices  27.3 us (16%)
  between operations  14.3 us (8%)
  local copies, waits for them, and re-layouts  3.22 us (2%)
  other arithmetic  2.77 us (2%)
    all_to_all x2, blocking collectives, exchange(): return lax.all_to_all(array, 'row', 0, 0, axis_index_groups=groups)  33.6 us
    pallas_call x4, Pallas kernels, factor_step(): pl.pallas_call(functools.partial(factor_kernel, d), in_specs=[IN_VMEM] *...  17.3 us
    all_to_all x1, waiting for transfers between devices, exchange(): return lax.all_to_all(array, 'row', 0, 0, axis_index_groups=groups)  17.2 us
    pallas_call x2, Pallas kernels, sketch_product(): pl.pallas_call(functools.partial(sketch_kernel, pieces), in_specs=[IN_SME...  16.4 us
    pallas_call x1, Pallas kernels, chip_products(): pl.pallas_call(chip_kernel, in_specs=[IN_SMEM] * 2 + [IN_VMEM] * 2 + [IN_...  12.2 us
    ppermute x3, starting transfers between devices, swap_core(): return lax.ppermute(array, 'row', row_pairs(lambda z, x, c: (z, x, 1 - c)))  11.8 us
    ppermute x8, starting transfers between devices, send_y(): return lax.ppermute(array, 'col', [(i, (i + step) % YS) for i in range(YS)])  11.1 us
    all_to_all x1, blocking collectives, shards(): gram = lax.all_to_all(repeat(gram, YS), 'col', 0, 0)  11 us
  transfers between devices with their start and end apart: 13, of which 6 were waited for; matrix products, arithmetic and copies ran while one was open for 2% of the time, Pallas kernels for 20%

profile of v3, /device:TPU:1, one launch (start us, length us, event | category | flops | bytes accessed | tf_op | source)
XLA Modules:
  0.0 170.7 jit_solution(11579123324774498741)
XLA Ops:
  7.2 3.3 %collective-permute-start.9 = (f32[512,4096]{1,0:T(8,128)}, f32[512,4096]{1,0:T(8,128)}, u32[]{:S(2)}, u32[]{:S(2)}) collective-permute-start(f32[512,4096]{1,0:T(8,128)} %panel_ref.3), channel_id=1, source_target_pairs={{0,4},{4,0},{8,12},{12,8},{16,20},{20,16},{24,28},{28,24},{32,36},... | collective-permute-start | bytes 25165832 | tf_op jit(solution)/shard_map/sketch/ppermute | solution.py:40
  10.5 8.4 %sketch_product.2 = (f32[128,512]{1,0:T(8,128)}, f32[128,512]{1,0:T(8,128)}) custom-call(s32[1]{0:T(128)} %bitcast.y_ref, f32[512,4096]{1,0:T(8,128)} %panel_ref.3, f32[4096,512]{1,0:T(8,128)} %matrix_ref.3), custom_call_target="tpu_custom_call" | custom-call | flops 3221225472 | bytes 12582912 | tf_op jit(solution)/shard_map/sketch/sketch_product/pallas_call | solution.py:148
  19.0 2.7 %collective-permute-start.1 = (f32[128,512]{1,0:T(8,128)}, f32[128,512]{1,0:T(8,128)S(1)}, u32[]{:S(2)}, u32[]{:S(2)}) collective-permute-start(f32[128,512]{1,0:T(8,128)} %get-tuple-element.33), channel_id=1, source_target_pairs={{0,3},{1,0},{2,1},{3,2},{4,7},{5,4},{6,5},{7,6},{8,11},{9,8},{10,9... | collective-permute-start | bytes 786440 | tf_op jit(solution)/shard_map/sketch/ppermute | solution.py:36
  21.7 8.1 %sketch_product.3 = (f32[64,512]{1,0:T(8,128)}, f32[64,512]{1,0:T(8,128)}, f32[128,512]{1,0:T(8,128)}) custom-call(s32[1]{0:T(128)} %bitcast.y_ref, f32[512,4096]{1,0:T(8,128)} %panel_ref.3, f32[4096,512]{1,0:T(8,128)} %matrix_ref.3), custom_call_target="tpu_custom_call" | custom-call | flops 3221225472 | bytes 12582912 | tf_op jit(solution)/shard_map/sketch/sketch_product/pallas_call | solution.py:148
  30.9 2.7 %collective-permute-start.3 = (f32[64,512]{1,0:T(8,128)S(1)}, f32[64,512]{1,0:T(8,128)S(1)}, u32[]{:S(2)}, u32[]{:S(2)}) collective-permute-start(f32[64,512]{1,0:T(8,128)S(1)} %get-tuple-element.39), channel_id=1, source_target_pairs={{0,3},{1,0},{2,1},{3,2},{4,7},{5,4},{6,5},{7,6},{8,11},{9,8},{10,9... | collective-permute-start | bytes 393224 | tf_op jit(solution)/shard_map/sketch/ppermute | solution.py:36
  33.5 3.0 %collective-permute-done.2 = f32[64,512]{1,0:T(8,128)S(1)} collective-permute-done((f32[64,512]{1,0:T(8,128)S(1)}, f32[64,512]{1,0:T(8,128)S(1)}, u32[]{:S(2)}, u32[]{:S(2)}) %collective-permute-start.2) | collective-permute-done | bytes 131104 | tf_op jit(solution)/shard_map/sketch/ppermute | solution.py:36
  37.7 2.7 %collective-permute-start.5 = (f32[128,512]{1,0:T(8,128)S(1)}, f32[128,512]{1,0:T(8,128)S(1)}, u32[]{:S(2)}, u32[]{:S(2)}) collective-permute-start(f32[128,512]{1,0:T(8,128)S(1)} %maximum_add_fusion.own), channel_id=1, source_target_pairs={{0,3},{1,0},{2,1},{3,2},{4,7},{5,4},{6,5},{7,6},{8,11},{9,8},{10,9... | collective-permute-start | bytes 786440 | tf_op jit(solution)/shard_map/sketch/ppermute | solution.py:36
  40.3 4.9 %collective-permute-done.4.before = f32[128,512]{1,0:T(8,128)S(1)} collective-permute-done((f32[128,512]{1,0:T(8,128)S(1)}, f32[128,512]{1,0:T(8,128)S(1)}, u32[]{:S(2)}, u32[]{:S(2)}) %collective-permute-start.4) | collective-permute-done | bytes 262176 | tf_op jit(solution)/shard_map/sketch/ppermute | solution.py:36
  45.5 2.5 %collective-permute-start.7 = (f32[64,512]{1,0:T(8,128)S(1)}, f32[64,512]{1,0:T(8,128)S(1)}, u32[]{:S(2)}, u32[]{:S(2)}) collective-permute-start(f32[64,512]{1,0:T(8,128)S(1)} %slice.23), channel_id=1, source_target_pairs={{0,3},{1,0},{2,1},{3,2},{4,7},{5,4},{6,5},{7,6},{8,11},{9,8},{10,9... | collective-permute-start | bytes 393224 | tf_op jit(solution)/shard_map/sketch/ppermute | solution.py:36
  48.1 2.3 %collective-permute-done.6.head = f32[64,512]{1,0:T(8,128)S(1)} collective-permute-done((f32[64,512]{1,0:T(8,128)S(1)}, f32[64,512]{1,0:T(8,128)S(1)}, u32[]{:S(2)}, u32[]{:S(2)}) %collective-permute-start.6) | collective-permute-done | bytes 131104 | tf_op jit(solution)/shard_map/sketch/ppermute | solution.py:36
  50.4 3.6 %collective-permute-start.8 = (f32[512,512]{1,0:T(8,128)S(1)}, f32[512,512]{1,0:T(8,128)S(1)}, u32[]{:S(2)}, u32[]{:S(2)}) collective-permute-start(f32[512,512]{1,0:T(8,128)S(1)} %bitcast.20), channel_id=1, source_target_pairs={{0,4},{4,0},{8,12},{12,8},{16,20},{20,16},{24,28},{28,24},{32,36},... | collective-permute-start | bytes 3145736 | tf_op jit(solution)/shard_map/sketch/ppermute | solution.py:40
  54.0 2.3 %collective-permute-done.8.other_ref = f32[512,512]{1,0:T(8,128)S(1)} collective-permute-done((f32[512,512]{1,0:T(8,128)S(1)}, f32[512,512]{1,0:T(8,128)S(1)}, u32[]{:S(2)}, u32[]{:S(2)}) %collective-permute-start.8) | collective-permute-done | bytes 1048608 | tf_op jit(solution)/shard_map/sketch/ppermute | solution.py:40
  57.3 12.2 %chip_products.1 = (f32[32,2,512]{2,1,0:T(2,128)}, f32[2048,512]{1,0:T(8,128)}) custom-call(s32[1]{0:T(128)} %bitcast.y_ref, s32[1]{0:T(128)} %bitcast.1.core_ref, f32[512,512]{1,0:T(8,128)} %bitcast.21, f32[512,512]{1,0:T(8,128)} %copy-done.2, f32[512,4096]{1,0:T(8,128)} %panel_ref.3, f32[512,4096]{1,0:T(8,128)} %collective-permute-done.9.arrived_ref), custom_call_target="tpu_custom_call" | custom-call | flops 6442450944 | bytes 25165824 | tf_op jit(solution)/shard_map/project/chip_products/pallas_call | solution.py:247
  69.5 19.0 %all_to_all.20 = f32[32,2,512]{2,1,0:T(2,128)S(1)} all-to-all(f32[32,2,512]{2,1,0:T(2,128)} %get-tuple-element.45), channel_id=1, replica_groups={{0,8,16,24,32,40,48,56,64,72,80,88,96,104,112,120,128,136,144,152,160,1..., dimensions={0} | all-to-all | bytes 262144 | tf_op jit(solution)/shard_map/gram/all_to_all | solution.py:44
  88.6 14.6 %all_to_all.21 = f32[32,2,512]{2,1,0:T(2,128)S(1)} all-to-all(f32[32,2,512]{2,1,0:T(2,128)S(1)} %broadcast_in_dim.24), channel_id=1, replica_groups={{0,8,16,24,32,40,48,56,64,72,80,88,96,104,112,120,128,136,144,152,160,1..., dimensions={0} | all-to-all | bytes 262144 | tf_op jit(solution)/shard_map/gram/all_to_all | solution.py:44
  103.4 11.0 %all_to_all.22 = f32[4,64,512]{2,1,0:T(8,128)S(1)} all-to-all(f32[4,64,512]{2,1,0:T(8,128)S(1)} %broadcast_in_dim.26), channel_id=1, replica_groups=mesh['row'=64,'col'=4] {'col'}, dimensions={0} | all-to-all | bytes 1048576 | tf_op jit(solution)/shard_map/gram/all_to_all | solution.py:452
  114.4 4.8 %collective-permute-start.10 = (f32[4,64,512]{2,1,0:T(8,128)S(1)}, f32[4,64,512]{2,1,0:T(8,128)S(1)}, u32[]{:S(2)}, u32[]{:S(2)}) collective-permute-start(f32[4,64,512]{2,1,0:T(8,128)S(1)} %all_to_all.22), channel_id=1, source_target_pairs={{0,4},{4,0},{8,12},{12,8},{16,20},{20,16},{24,28},{28,24},{32,36},... | collective-permute-start | bytes 1572872 | tf_op jit(solution)/shard_map/gram/ppermute | solution.py:40
  120.8 4.1 %factor_step.4 = (f32[128,512]{1,0:T(8,128)S(1)}, f32[128,512]{1,0:T(8,128)S(1)}) custom-call(f32[512,512]{1,0:T(8,128)S(1)} %bitcast.22), custom_call_target="tpu_custom_call" | custom-call | flops 5000000000 | bytes 786432 | tf_op jit(solution)/shard_map/factor/factor_step/pallas_call | solution.py:361
  124.9 4.3 %factor_step.5 = (f32[128,512]{1,0:T(8,128)S(1)}, f32[128,512]{1,0:T(8,128)S(1)}) custom-call(f32[512,512]{1,0:T(8,128)S(1)} %bitcast.23, f32[128,512]{1,0:T(8,128)S(1)} %get-tuple-element.47.refs_1_, f32[128,512]{1,0:T(8,128)S(1)} %get-tuple-element.46.refs_2_.refs_3_.refs_4_.refs_0_), custom_call_target="tpu_custom_call" | custom-call | flops 5000000000 | bytes 1310720 | tf_op jit(solution)/shard_map/factor/factor_step/pallas_call | solution.py:361
  129.2 4.4 %factor_step.6 = (f32[128,512]{1,0:T(8,128)S(1)}, f32[128,512]{1,0:T(8,128)S(1)}) custom-call(f32[512,512]{1,0:T(8,128)S(1)} %bitcast.24, f32[128,512]{1,0:T(8,128)S(1)} %get-tuple-element.47.refs_1_, f32[128,512]{1,0:T(8,128)S(1)} %get-tuple-element.49.refs_2_, f32[128,512]{1,0:T(8,128)S(1)} %get-tuple-element.46.refs_2_.refs_3_.refs_4_.refs_0_, ...), custom_call_target="tpu_custom_call" | custom-call | flops 5000000000 | bytes 1835008 | tf_op jit(solution)/shard_map/factor/factor_step/pallas_call | solution.py:361
  133.6 4.5 %factor_step.7 = (f32[128,512]{1,0:T(8,128)S(1)}, f32[128,512]{1,0:T(8,128)S(1)}) custom-call(f32[512,512]{1,0:T(8,128)S(1)} %bitcast.25, f32[128,512]{1,0:T(8,128)S(1)} %get-tuple-element.47.refs_1_, f32[128,512]{1,0:T(8,128)S(1)} %get-tuple-element.49.refs_2_, f32[128,512]{1,0:T(8,128)S(1)} %get-tuple-element.51.refs_3_, ...), custom_call_target="tpu_custom_call" | custom-call | flops 5000000000 | bytes 2359296 | tf_op jit(solution)/shard_map/factor/factor_step/pallas_call | solution.py:361
  139.2 1.6 apply_inverse.1
  140.7 4.4 %all-to-all-start.3 = ((f32[64,8,256]{2,1,0:T(8,128)}), f32[64,8,256]{2,1,0:T(8,128)S(1)}, u32[]{:S(2)}, u32[]{:S(2)}) async-start(f32[64,8,256]{2,1,0:T(8,128)} %bitcast.9), calls=%async_computation.4 | async-start | bytes 1048576 | tf_op jit(solution)/shard_map/apply/all_to_all | solution.py:44
  145.8 17.2 %all-to-all-done.3 = f32[64,8,256]{2,1,0:T(8,128)S(1)} async-done(((f32[64,8,256]{2,1,0:T(8,128)}), f32[64,8,256]{2,1,0:T(8,128)S(1)}, u32[]{:S(2)}, u32[]{:S(2)}) %all-to-all-start.3) | async-done | bytes 524320 | tf_op jit(solution)/shard_map/apply/all_to_all | solution.py:44
  (38 shorter events, 8.1 us)
Async XLA Ops:
  7.2 131.0 %reduce-scatter.2.cloned.1.call-start = ((), (), s32[]{:S(2)}) async-start(), calls=%async_computation.5 | async-start | bytes 4718592 | tf_op jit(solution)/shard_map/project/reduce_scatter | solution.py:445
  7.2 49.1 %collective-permute-start.9 = (f32[512,4096]{1,0:T(8,128)}, f32[512,4096]{1,0:T(8,128)}, u32[]{:S(2)}, u32[]{:S(2)}) collective-permute-start(f32[512,4096]{1,0:T(8,128)} %panel_ref.3), channel_id=1, source_target_pairs={{0,4},{4,0},{8,12},{12,8},{16,20},{20,16},{24,28},{28,24},{32,36},... | collective-permute-start | bytes 25165832 | tf_op jit(solution)/shard_map/sketch/ppermute | solution.py:40
  18.9 10.8 %collective-permute-start = (f32[128,512]{1,0:T(8,128)}, f32[128,512]{1,0:T(8,128)S(1)}, u32[]{:S(2)}, u32[]{:S(2)}) collective-permute-start(f32[128,512]{1,0:T(8,128)} %get-tuple-element.32), channel_id=1, source_target_pairs={{0,1},{1,2},{2,3},{3,0},{4,5},{5,6},{6,7},{7,4},{8,9},{9,10},{10,1... | collective-permute-start | bytes 786440 | tf_op jit(solution)/shard_map/sketch/ppermute | solution.py:36
  19.0 10.8 %collective-permute-start.1 = (f32[128,512]{1,0:T(8,128)}, f32[128,512]{1,0:T(8,128)S(1)}, u32[]{:S(2)}, u32[]{:S(2)}) collective-permute-start(f32[128,512]{1,0:T(8,128)} %get-tuple-element.33), channel_id=1, source_target_pairs={{0,3},{1,0},{2,1},{3,2},{4,7},{5,4},{6,5},{7,6},{8,11},{9,8},{10,9... | collective-permute-start | bytes 786440 | tf_op jit(solution)/shard_map/sketch/ppermute | solution.py:36
  30.8 5.7 %collective-permute-start.2 = (f32[64,512]{1,0:T(8,128)S(1)}, f32[64,512]{1,0:T(8,128)S(1)}, u32[]{:S(2)}, u32[]{:S(2)}) collective-permute-start(f32[64,512]{1,0:T(8,128)S(1)} %get-tuple-element.38), channel_id=1, source_target_pairs={{0,1},{1,2},{2,3},{3,0},{4,5},{5,6},{6,7},{7,4},{8,9},{9,10},{10,1... | collective-permute-start | bytes 393224 | tf_op jit(solution)/shard_map/sketch/ppermute | solution.py:36
  30.9 5.7 %collective-permute-start.3 = (f32[64,512]{1,0:T(8,128)S(1)}, f32[64,512]{1,0:T(8,128)S(1)}, u32[]{:S(2)}, u32[]{:S(2)}) collective-permute-start(f32[64,512]{1,0:T(8,128)S(1)} %get-tuple-element.39), channel_id=1, source_target_pairs={{0,3},{1,0},{2,1},{3,2},{4,7},{5,4},{6,5},{7,6},{8,11},{9,8},{10,9... | collective-permute-start | bytes 393224 | tf_op jit(solution)/shard_map/sketch/ppermute | solution.py:36
  37.6 7.6 %collective-permute-start.4 = (f32[128,512]{1,0:T(8,128)S(1)}, f32[128,512]{1,0:T(8,128)S(1)}, u32[]{:S(2)}, u32[]{:S(2)}) collective-permute-start(f32[128,512]{1,0:T(8,128)S(1)} %maximum_add_fusion.own), channel_id=1, source_target_pairs={{0,1},{1,2},{2,3},{3,0},{4,5},{5,6},{6,7},{7,4},{8,9},{9,10},{10,1... | collective-permute-start | bytes 786440 | tf_op jit(solution)/shard_map/sketch/ppermute | solution.py:36
  37.7 7.5 %collective-permute-start.5 = (f32[128,512]{1,0:T(8,128)S(1)}, f32[128,512]{1,0:T(8,128)S(1)}, u32[]{:S(2)}, u32[]{:S(2)}) collective-permute-start(f32[128,512]{1,0:T(8,128)S(1)} %maximum_add_fusion.own), channel_id=1, source_target_pairs={{0,3},{1,0},{2,1},{3,2},{4,7},{5,4},{6,5},{7,6},{8,11},{9,8},{10,9... | collective-permute-start | bytes 786440 | tf_op jit(solution)/shard_map/sketch/ppermute | solution.py:36
  45.2 5.1 %collective-permute-start.6 = (f32[64,512]{1,0:T(8,128)S(1)}, f32[64,512]{1,0:T(8,128)S(1)}, u32[]{:S(2)}, u32[]{:S(2)}) collective-permute-start(f32[64,512]{1,0:T(8,128)S(1)} %slice.22), channel_id=1, source_target_pairs={{0,1},{1,2},{2,3},{3,0},{4,5},{5,6},{6,7},{7,4},{8,9},{9,10},{10,1... | collective-permute-start | bytes 393224 | tf_op jit(solution)/shard_map/sketch/ppermute | solution.py:36
  45.5 4.8 %collective-permute-start.7 = (f32[64,512]{1,0:T(8,128)S(1)}, f32[64,512]{1,0:T(8,128)S(1)}, u32[]{:S(2)}, u32[]{:S(2)}) collective-permute-start(f32[64,512]{1,0:T(8,128)S(1)} %slice.23), channel_id=1, source_target_pairs={{0,3},{1,0},{2,1},{3,2},{4,7},{5,4},{6,5},{7,6},{8,11},{9,8},{10,9... | collective-permute-start | bytes 393224 | tf_op jit(solution)/shard_map/sketch/ppermute | solution.py:36
  50.4 5.9 %copy-start = (f32[4,128,512]{2,1,0:T(8,128)}, f32[4,128,512]{2,1,0:T(8,128)S(1)}, u32[]{:S(2)}) copy-start(f32[4,128,512]{2,1,0:T(8,128)S(1)} %place_blocks.1) | copy-start | bytes 3145732
  50.4 5.9 %collective-permute-start.8 = (f32[512,512]{1,0:T(8,128)S(1)}, f32[512,512]{1,0:T(8,128)S(1)}, u32[]{:S(2)}, u32[]{:S(2)}) collective-permute-start(f32[512,512]{1,0:T(8,128)S(1)} %bitcast.20), channel_id=1, source_target_pairs={{0,4},{4,0},{8,12},{12,8},{16,20},{20,16},{24,28},{28,24},{32,36},... | collective-permute-start | bytes 3145736 | tf_op jit(solution)/shard_map/sketch/ppermute | solution.py:40
  56.3 1.0 copy-start.2
  114.4 6.4 %collective-permute-start.10 = (f32[4,64,512]{2,1,0:T(8,128)S(1)}, f32[4,64,512]{2,1,0:T(8,128)S(1)}, u32[]{:S(2)}, u32[]{:S(2)}) collective-permute-start(f32[4,64,512]{2,1,0:T(8,128)S(1)} %all_to_all.22), channel_id=1, source_target_pairs={{0,4},{4,0},{8,12},{12,8},{16,20},{20,16},{24,28},{28,24},{32,36},... | collective-permute-start | bytes 1572872 | tf_op jit(solution)/shard_map/gram/ppermute | solution.py:40
  138.1 1.0 copy-start.1
  140.7 22.3 %all-to-all-start.3 = ((f32[64,8,256]{2,1,0:T(8,128)}), f32[64,8,256]{2,1,0:T(8,128)S(1)}, u32[]{:S(2)}, u32[]{:S(2)}) async-start(f32[64,8,256]{2,1,0:T(8,128)} %bitcast.9), calls=%async_computation.4 | async-start | bytes 1048576 | tf_op jit(solution)/shard_map/apply/all_to_all | solution.py:44
Sparse Core Ops, SparseCore 0:
  69.6 60.0 reduce-scatter.1

commit v4 on v3

--- a/solution.py
+++ b/solution.py
@@ -319,9 +319,25 @@
     return out
 
 
-def factor_kernel(d, *refs):
+def apply_block(d, rows_ref, total, scale, out_ref):
+    end = BLOCK * (d + 1)
+    rows = split(rows_ref[:, :end])
+    term = lambda i, j: lax.dot_general(
+        rows[i], total[j][:, :end], (((1,), (1,)), ((), ())), preferred_element_type=F32
+    )
+    out_ref[BLOCK * d : end, :] = (term(0, 0) + term(0, 1) + term(1, 0)) * scale
+
+
+def factor_kernel(d, scale, *refs):
     gram_ref, upper, inverse = refs[0], refs[1 : 1 + d], refs[1 + d : 1 + 2 * d]
-    upper_ref, inverse_ref, work = refs[1 + 2 * d :]
+    work, refs = refs[-1], refs[1 + 2 * d : -1]
+    if scale is None:
+        upper_ref, inverse_ref = refs
+    else:
+        total_ref, upper_ref, inverse_ref, result_ref = refs
+        total = split(total_ref[...])
+        for k in range(d):
+            apply_block(k, inverse[k], total, scale, result_ref)
     rank = gram_ref.shape[1]
     low = BLOCK * d
     here = slice(low, low + BLOCK)
@@ -353,59 +369,39 @@
         upper_ref[:, low + BLOCK :] = block_dot(block_inverse, right[:, BLOCK:], ((1,), (0,)))
     if d:
         inverse_ref[:, :low] = block_dot(block_inverse, left, ((1,), (0,)))
-
-
-def factor_step(d, gram, upper, inverse):
+    if scale is not None:
+        apply_block(d, inverse_ref, total, scale, result_ref)
+
+
+def factor_step(d, gram, upper, inverse, total=None, scale=None):
     rank = gram.shape[1]
-    out = jax.ShapeDtypeStruct((BLOCK, rank), F32)
+    operands = [gram, *upper, *inverse]
+    outs = [jax.ShapeDtypeStruct((BLOCK, rank), F32)] * 2
+    if total is not None:
+        operands.append(total)
+        outs.append(jax.ShapeDtypeStruct((rank, total.shape[0]), F32))
     return pl.pallas_call(
-        functools.partial(factor_kernel, d),
-        in_specs=[IN_VMEM] * (1 + 2 * d),
-        out_specs=(IN_VMEM, IN_VMEM),
-        out_shape=(out, out),
+        functools.partial(factor_kernel, d, scale),
+        in_specs=[IN_VMEM] * len(operands),
+        out_specs=[IN_VMEM] * len(outs),
+        out_shape=outs,
         scratch_shapes=[pltpu.VMEM((BLOCK, 2 * BLOCK), F32)],
         compiler_params=params(24),
         cost_estimate=cost(5_000_000_000, 4 * BLOCK * rank * (2 * d + 3)),
         name="factor_step",
-    )(gram, *upper, *inverse)
-
-
-def factorize(gram):
+    )(*operands)
+
+
+def factorize(gram, total, scale):
     upper, inverse = [], []
-    for d in range(gram.shape[0] // BLOCK):
+    last = gram.shape[0] // BLOCK - 1
+    for d in range(last):
         up, inv = factor_step(d, gram, upper, inverse)
         upper.append(up)
         inverse.append(inv)
-    return jnp.concatenate(upper, 0), inverse
-
-
-def apply_kernel(scale, total_ref, *refs):
-    inverse, (out_ref, total, sem) = refs[:-3], refs[-3:]
-    load = pltpu.make_async_copy(total_ref, total, sem)
-    load.start()
-    load.wait()
-    high, low = split(total[...])
-    across = lambda a, b: lax.dot_general(a, b, (((1,), (1,)), ((), ())), preferred_element_type=F32)
-    for d, rows_ref in enumerate(inverse):
-        end = BLOCK * (d + 1)
-        rows_high, rows_low = split(rows_ref[:, :end])
-        term = across(rows_high, high[:, :end])
-        term += across(rows_high, low[:, :end]) + across(rows_low, high[:, :end])
-        out_ref[BLOCK * d : end, :] = term * scale
-
-
-def apply_inverse(inverse, total, scale):
-    cols, rank = total.shape
-    return pl.pallas_call(
-        functools.partial(apply_kernel, scale),
-        in_specs=[IN_PLACE] + [IN_VMEM] * len(inverse),
-        out_specs=IN_VMEM,
-        out_shape=jax.ShapeDtypeStruct((rank, cols), F32),
-        scratch_shapes=[pltpu.VMEM((cols, rank), F32), pltpu.SemaphoreType.DMA],
-        compiler_params=params(24),
-        cost_estimate=cost(6 * rank * rank * cols, 8 * rank * (rank + cols)),
-        name="apply_inverse",
-    )(total, *inverse)
+    gram, total = together(gram, total)
+    up, _, result = factor_step(last, gram, upper, inverse, total, scale)
+    return jnp.concatenate([*upper, up], 0), result
 
 
 def shards(panel, sketch_matrix):
@@ -454,10 +450,9 @@
         gram = gram.transpose(1, 0, 2, 3).reshape(rank, rank)
 
     with jax.named_scope("factor"):
-        upper, inverse = factorize(gram)
+        upper, result = factorize(gram, total, norm_scale)
 
     with jax.named_scope("apply"):
-        result = apply_inverse(inverse, total, norm_scale)
         result = exchange(result.reshape(ZS * XS * CS, row_share, -1), None)
         result = result.reshape(ZS, XS, CS, row_share, -1).sum(1)
         projected = result.transpose(2, 1, 0, 3).reshape(row_share, local_cols)

time: 171 us -> 171 us (level)
    pallas_call x5 -> x4, Pallas kernels: 18.9 us -> 19 us  [factor_step(): pl.pallas_call(functools.partial(factor_kernel, d, scale), in_specs=[IN_V...]
  transfers between devices with their start and end apart: 13 -> 13, of which waited for: 6 -> 6; matrix products, arithmetic and copies ran while one was open for 2% -> 2% of each run, Pallas kernels for 20% -> 17%
where the time goes in v4:
time: 171 us
  Pallas kernels  47.8 us (28%)
  blocking collectives  44.6 us (26%)
  waiting for transfers between devices  31 us (18%)
  starting transfers between devices  27.3 us (16%)
  between operations  14.2 us (8%)
  local copies, waits for them, and re-layouts  3.22 us (2%)
  other arithmetic  2.77 us (2%)
    all_to_all x2, blocking collectives, exchange(): return lax.all_to_all(array, 'row', 0, 0, axis_index_groups=groups)  33.6 us
    pallas_call x4, Pallas kernels, factor_step(): pl.pallas_call(functools.partial(factor_kernel, d, scale), in_specs=[IN_V...  19 us
    all_to_all x1, waiting for transfers between devices, exchange(): return lax.all_to_all(array, 'row', 0, 0, axis_index_groups=groups)  17.2 us
    pallas_call x2, Pallas kernels, sketch_product(): pl.pallas_call(functools.partial(sketch_kernel, pieces), in_specs=[IN_SME...  16.4 us
    pallas_call x1, Pallas kernels, chip_products(): pl.pallas_call(chip_kernel, in_specs=[IN_SMEM] * 2 + [IN_VMEM] * 2 + [IN_...  12.2 us
    ppermute x3, starting transfers between devices, swap_core(): return lax.ppermute(array, 'row', row_pairs(lambda z, x, c: (z, x, 1 - c)))  11.8 us
    ppermute x8, starting transfers between devices, send_y(): return lax.ppermute(array, 'col', [(i, (i + step) % YS) for i in range(YS)])  11.1 us
    all_to_all x1, blocking collectives, shards(): gram = lax.all_to_all(repeat(gram, YS), 'col', 0, 0)  11 us
  transfers between devices with their start and end apart: 13, of which 6 were waited for; matrix products, arithmetic and copies ran while one was open for 2% of the time, Pallas kernels for 17%

profile of v4, /device:TPU:1, one launch (start us, length us, event | category | flops | bytes accessed | tf_op | source)
XLA Modules:
  0.0 170.9 jit_solution(9893031287699822552)
XLA Ops:
  7.2 3.3 %collective-permute-start.9 = (f32[512,4096]{1,0:T(8,128)}, f32[512,4096]{1,0:T(8,128)}, u32[]{:S(2)}, u32[]{:S(2)}) collective-permute-start(f32[512,4096]{1,0:T(8,128)} %panel_ref.3), channel_id=1, source_target_pairs={{0,4},{4,0},{8,12},{12,8},{16,20},{20,16},{24,28},{28,24},{32,36},... | collective-permute-start | bytes 25165832 | tf_op jit(solution)/shard_map/sketch/ppermute | solution.py:40
  10.5 8.4 %sketch_product.2 = (f32[128,512]{1,0:T(8,128)}, f32[128,512]{1,0:T(8,128)}) custom-call(s32[1]{0:T(128)} %bitcast.y_ref, f32[512,4096]{1,0:T(8,128)} %panel_ref.3, f32[4096,512]{1,0:T(8,128)} %matrix_ref.3), custom_call_target="tpu_custom_call" | custom-call | flops 3221225472 | bytes 12582912 | tf_op jit(solution)/shard_map/sketch/sketch_product/pallas_call | solution.py:148
  19.0 2.7 %collective-permute-start.1 = (f32[128,512]{1,0:T(8,128)}, f32[128,512]{1,0:T(8,128)S(1)}, u32[]{:S(2)}, u32[]{:S(2)}) collective-permute-start(f32[128,512]{1,0:T(8,128)} %get-tuple-element.35), channel_id=1, source_target_pairs={{0,3},{1,0},{2,1},{3,2},{4,7},{5,4},{6,5},{7,6},{8,11},{9,8},{10,9... | collective-permute-start | bytes 786440 | tf_op jit(solution)/shard_map/sketch/ppermute | solution.py:36
  21.7 8.1 %sketch_product.3 = (f32[64,512]{1,0:T(8,128)}, f32[64,512]{1,0:T(8,128)}, f32[128,512]{1,0:T(8,128)}) custom-call(s32[1]{0:T(128)} %bitcast.y_ref, f32[512,4096]{1,0:T(8,128)} %panel_ref.3, f32[4096,512]{1,0:T(8,128)} %matrix_ref.3), custom_call_target="tpu_custom_call" | custom-call | flops 3221225472 | bytes 12582912 | tf_op jit(solution)/shard_map/sketch/sketch_product/pallas_call | solution.py:148
  30.9 2.7 %collective-permute-start.3 = (f32[64,512]{1,0:T(8,128)S(1)}, f32[64,512]{1,0:T(8,128)S(1)}, u32[]{:S(2)}, u32[]{:S(2)}) collective-permute-start(f32[64,512]{1,0:T(8,128)S(1)} %get-tuple-element.41), channel_id=1, source_target_pairs={{0,3},{1,0},{2,1},{3,2},{4,7},{5,4},{6,5},{7,6},{8,11},{9,8},{10,9... | collective-permute-start | bytes 393224 | tf_op jit(solution)/shard_map/sketch/ppermute | solution.py:36
  33.5 3.0 %collective-permute-done.2 = f32[64,512]{1,0:T(8,128)S(1)} collective-permute-done((f32[64,512]{1,0:T(8,128)S(1)}, f32[64,512]{1,0:T(8,128)S(1)}, u32[]{:S(2)}, u32[]{:S(2)}) %collective-permute-start.2) | collective-permute-done | bytes 131104 | tf_op jit(solution)/shard_map/sketch/ppermute | solution.py:36
  37.7 2.7 %collective-permute-start.5 = (f32[128,512]{1,0:T(8,128)S(1)}, f32[128,512]{1,0:T(8,128)S(1)}, u32[]{:S(2)}, u32[]{:S(2)}) collective-permute-start(f32[128,512]{1,0:T(8,128)S(1)} %maximum_add_fusion.own), channel_id=1, source_target_pairs={{0,3},{1,0},{2,1},{3,2},{4,7},{5,4},{6,5},{7,6},{8,11},{9,8},{10,9... | collective-permute-start | bytes 786440 | tf_op jit(solution)/shard_map/sketch/ppermute | solution.py:36
  40.3 4.9 %collective-permute-done.4.before = f32[128,512]{1,0:T(8,128)S(1)} collective-permute-done((f32[128,512]{1,0:T(8,128)S(1)}, f32[128,512]{1,0:T(8,128)S(1)}, u32[]{:S(2)}, u32[]{:S(2)}) %collective-permute-start.4) | collective-permute-done | bytes 262176 | tf_op jit(solution)/shard_map/sketch/ppermute | solution.py:36
  45.5 2.5 %collective-permute-start.7 = (f32[64,512]{1,0:T(8,128)S(1)}, f32[64,512]{1,0:T(8,128)S(1)}, u32[]{:S(2)}, u32[]{:S(2)}) collective-permute-start(f32[64,512]{1,0:T(8,128)S(1)} %slice.23), channel_id=1, source_target_pairs={{0,3},{1,0},{2,1},{3,2},{4,7},{5,4},{6,5},{7,6},{8,11},{9,8},{10,9... | collective-permute-start | bytes 393224 | tf_op jit(solution)/shard_map/sketch/ppermute | solution.py:36
  48.1 2.3 %collective-permute-done.6.head = f32[64,512]{1,0:T(8,128)S(1)} collective-permute-done((f32[64,512]{1,0:T(8,128)S(1)}, f32[64,512]{1,0:T(8,128)S(1)}, u32[]{:S(2)}, u32[]{:S(2)}) %collective-permute-start.6) | collective-permute-done | bytes 131104 | tf_op jit(solution)/shard_map/sketch/ppermute | solution.py:36
  50.4 3.6 %collective-permute-start.8 = (f32[512,512]{1,0:T(8,128)S(1)}, f32[512,512]{1,0:T(8,128)S(1)}, u32[]{:S(2)}, u32[]{:S(2)}) collective-permute-start(f32[512,512]{1,0:T(8,128)S(1)} %bitcast.20), channel_id=1, source_target_pairs={{0,4},{4,0},{8,12},{12,8},{16,20},{20,16},{24,28},{28,24},{32,36},... | collective-permute-start | bytes 3145736 | tf_op jit(solution)/shard_map/sketch/ppermute | solution.py:40
  54.0 2.3 %collective-permute-done.8.other_ref = f32[512,512]{1,0:T(8,128)S(1)} collective-permute-done((f32[512,512]{1,0:T(8,128)S(1)}, f32[512,512]{1,0:T(8,128)S(1)}, u32[]{:S(2)}, u32[]{:S(2)}) %collective-permute-start.8) | collective-permute-done | bytes 1048608 | tf_op jit(solution)/shard_map/sketch/ppermute | solution.py:40
  57.3 12.2 %chip_products.1 = (f32[32,2,512]{2,1,0:T(2,128)}, f32[2048,512]{1,0:T(8,128)}) custom-call(s32[1]{0:T(128)} %bitcast.y_ref, s32[1]{0:T(128)} %bitcast.1.core_ref, f32[512,512]{1,0:T(8,128)} %bitcast.21, f32[512,512]{1,0:T(8,128)} %copy-done.2, f32[512,4096]{1,0:T(8,128)} %panel_ref.3, f32[512,4096]{1,0:T(8,128)} %collective-permute-done.9.arrived_ref), custom_call_target="tpu_custom_call" | custom-call | flops 6442450944 | bytes 25165824 | tf_op jit(solution)/shard_map/project/chip_products/pallas_call | solution.py:247
  69.5 19.0 %all_to_all.20 = f32[32,2,512]{2,1,0:T(2,128)S(1)} all-to-all(f32[32,2,512]{2,1,0:T(2,128)} %get-tuple-element.46), channel_id=1, replica_groups={{0,8,16,24,32,40,48,56,64,72,80,88,96,104,112,120,128,136,144,152,160,1..., dimensions={0} | all-to-all | bytes 262144 | tf_op jit(solution)/shard_map/gram/all_to_all | solution.py:44
  88.6 14.6 %all_to_all.21 = f32[32,2,512]{2,1,0:T(2,128)S(1)} all-to-all(f32[32,2,512]{2,1,0:T(2,128)S(1)} %broadcast_in_dim.24), channel_id=1, replica_groups={{0,8,16,24,32,40,48,56,64,72,80,88,96,104,112,120,128,136,144,152,160,1..., dimensions={0} | all-to-all | bytes 262144 | tf_op jit(solution)/shard_map/gram/all_to_all | solution.py:44
  103.4 11.0 %all_to_all.22 = f32[4,64,512]{2,1,0:T(8,128)S(1)} all-to-all(f32[4,64,512]{2,1,0:T(8,128)S(1)} %broadcast_in_dim.26), channel_id=1, replica_groups=mesh['row'=64,'col'=4] {'col'}, dimensions={0} | all-to-all | bytes 1048576 | tf_op jit(solution)/shard_map/gram/all_to_all | solution.py:448
  114.4 4.8 %collective-permute-start.10 = (f32[4,64,512]{2,1,0:T(8,128)S(1)}, f32[4,64,512]{2,1,0:T(8,128)S(1)}, u32[]{:S(2)}, u32[]{:S(2)}) collective-permute-start(f32[4,64,512]{2,1,0:T(8,128)S(1)} %all_to_all.22), channel_id=1, source_target_pairs={{0,4},{4,0},{8,12},{12,8},{16,20},{20,16},{24,28},{28,24},{32,36},... | collective-permute-start | bytes 1572872 | tf_op jit(solution)/shard_map/gram/ppermute | solution.py:40
  119.4 1.4 collective-permute-done.10
  120.8 4.1 %factor_step.4 = (f32[128,512]{1,0:T(8,128)S(1)}, f32[128,512]{1,0:T(8,128)S(1)}) custom-call(f32[512,512]{1,0:T(8,128)S(1)} %bitcast.22), custom_call_target="tpu_custom_call" | custom-call | flops 5000000000 | bytes 786432 | tf_op jit(solution)/shard_map/factor/factor_step/pallas_call | solution.py:383
  124.8 4.3 %factor_step.5 = (f32[128,512]{1,0:T(8,128)S(1)}, f32[128,512]{1,0:T(8,128)S(1)}) custom-call(f32[512,512]{1,0:T(8,128)S(1)} %bitcast.23, f32[128,512]{1,0:T(8,128)S(1)} %get-tuple-element.49.refs_1_, f32[128,512]{1,0:T(8,128)S(1)} %get-tuple-element.50.refs_2_.refs_3_.refs_4_), custom_call_target="tpu_custom_call" | custom-call | flops 5000000000 | bytes 1310720 | tf_op jit(solution)/shard_map/factor/factor_step/pallas_call | solution.py:383
  129.2 4.4 %factor_step.6 = (f32[128,512]{1,0:T(8,128)S(1)}, f32[128,512]{1,0:T(8,128)S(1)}) custom-call(f32[512,512]{1,0:T(8,128)S(1)} %bitcast.24, f32[128,512]{1,0:T(8,128)S(1)} %get-tuple-element.49.refs_1_, f32[128,512]{1,0:T(8,128)S(1)} %get-tuple-element.51.refs_2_, f32[128,512]{1,0:T(8,128)S(1)} %get-tuple-element.50.refs_2_.refs_3_.refs_4_, ...), custom_call_target="tpu_custom_call" | custom-call | flops 5000000000 | bytes 1835008 | tf_op jit(solution)/shard_map/factor/factor_step/pallas_call | solution.py:383
  134.7 6.2 %factor_step.7 = (f32[128,512]{1,0:T(8,128)S(1)}, f32[128,512]{1,0:T(8,128)}, f32[512,256]{1,0:T(8,128)}) custom-call(f32[512,512]{1,0:T(8,128)S(1)} %bitcast.25, f32[128,512]{1,0:T(8,128)S(1)} %get-tuple-element.49.refs_1_, f32[128,512]{1,0:T(8,128)S(1)} %get-tuple-element.51.refs_2_, f32[128,512]{1,0:T(8,128)S(1)} %get-tuple-element.53.refs_3_, ...), custom_call_target="tpu_custom_call" | custom-call | flops 5000000000 | bytes 2359296 | tf_op jit(solution)/shard_map/factor/factor_step/pallas_call | solution.py:383
  140.9 4.4 %all-to-all-start.3 = ((f32[64,8,256]{2,1,0:T(8,128)}), f32[64,8,256]{2,1,0:T(8,128)S(1)}, u32[]{:S(2)}, u32[]{:S(2)}) async-start(f32[64,8,256]{2,1,0:T(8,128)} %bitcast.9), calls=%async_computation.4 | async-start | bytes 1048576 | tf_op jit(solution)/shard_map/apply/all_to_all | solution.py:44
  146.0 17.2 %all-to-all-done.3 = f32[64,8,256]{2,1,0:T(8,128)S(1)} async-done(((f32[64,8,256]{2,1,0:T(8,128)}), f32[64,8,256]{2,1,0:T(8,128)S(1)}, u32[]{:S(2)}, u32[]{:S(2)}) %all-to-all-start.3) | async-done | bytes 524320 | tf_op jit(solution)/shard_map/apply/all_to_all | solution.py:44
  (37 shorter events, 6.7 us)
Async XLA Ops:
  7.2 126.5 %reduce-scatter.2.cloned.1.call-start = ((), (), s32[]{:S(2)}) async-start(), calls=%async_computation.5 | async-start | bytes 4718592 | tf_op jit(solution)/shard_map/project/reduce_scatter | solution.py:441
  7.2 49.1 %collective-permute-start.9 = (f32[512,4096]{1,0:T(8,128)}, f32[512,4096]{1,0:T(8,128)}, u32[]{:S(2)}, u32[]{:S(2)}) collective-permute-start(f32[512,4096]{1,0:T(8,128)} %panel_ref.3), channel_id=1, source_target_pairs={{0,4},{4,0},{8,12},{12,8},{16,20},{20,16},{24,28},{28,24},{32,36},... | collective-permute-start | bytes 25165832 | tf_op jit(solution)/shard_map/sketch/ppermute | solution.py:40
  18.9 10.8 %collective-permute-start = (f32[128,512]{1,0:T(8,128)}, f32[128,512]{1,0:T(8,128)S(1)}, u32[]{:S(2)}, u32[]{:S(2)}) collective-permute-start(f32[128,512]{1,0:T(8,128)} %get-tuple-element.34), channel_id=1, source_target_pairs={{0,1},{1,2},{2,3},{3,0},{4,5},{5,6},{6,7},{7,4},{8,9},{9,10},{10,1... | collective-permute-start | bytes 786440 | tf_op jit(solution)/shard_map/sketch/ppermute | solution.py:36
  19.0 10.8 %collective-permute-start.1 = (f32[128,512]{1,0:T(8,128)}, f32[128,512]{1,0:T(8,128)S(1)}, u32[]{:S(2)}, u32[]{:S(2)}) collective-permute-start(f32[128,512]{1,0:T(8,128)} %get-tuple-element.35), channel_id=1, source_target_pairs={{0,3},{1,0},{2,1},{3,2},{4,7},{5,4},{6,5},{7,6},{8,11},{9,8},{10,9... | collective-permute-start | bytes 786440 | tf_op jit(solution)/shard_map/sketch/ppermute | solution.py:36
  30.8 5.7 %collective-permute-start.2 = (f32[64,512]{1,0:T(8,128)S(1)}, f32[64,512]{1,0:T(8,128)S(1)}, u32[]{:S(2)}, u32[]{:S(2)}) collective-permute-start(f32[64,512]{1,0:T(8,128)S(1)} %get-tuple-element.40), channel_id=1, source_target_pairs={{0,1},{1,2},{2,3},{3,0},{4,5},{5,6},{6,7},{7,4},{8,9},{9,10},{10,1... | collective-permute-start | bytes 393224 | tf_op jit(solution)/shard_map/sketch/ppermute | solution.py:36
  30.9 5.7 %collective-permute-start.3 = (f32[64,512]{1,0:T(8,128)S(1)}, f32[64,512]{1,0:T(8,128)S(1)}, u32[]{:S(2)}, u32[]{:S(2)}) collective-permute-start(f32[64,512]{1,0:T(8,128)S(1)} %get-tuple-element.41), channel_id=1, source_target_pairs={{0,3},{1,0},{2,1},{3,2},{4,7},{5,4},{6,5},{7,6},{8,11},{9,8},{10,9... | collective-permute-start | bytes 393224 | tf_op jit(solution)/shard_map/sketch/ppermute | solution.py:36
  37.6 7.6 %collective-permute-start.4 = (f32[128,512]{1,0:T(8,128)S(1)}, f32[128,512]{1,0:T(8,128)S(1)}, u32[]{:S(2)}, u32[]{:S(2)}) collective-permute-start(f32[128,512]{1,0:T(8,128)S(1)} %maximum_add_fusion.own), channel_id=1, source_target_pairs={{0,1},{1,2},{2,3},{3,0},{4,5},{5,6},{6,7},{7,4},{8,9},{9,10},{10,1... | collective-permute-start | bytes 786440 | tf_op jit(solution)/shard_map/sketch/ppermute | solution.py:36
  37.7 7.5 %collective-permute-start.5 = (f32[128,512]{1,0:T(8,128)S(1)}, f32[128,512]{1,0:T(8,128)S(1)}, u32[]{:S(2)}, u32[]{:S(2)}) collective-permute-start(f32[128,512]{1,0:T(8,128)S(1)} %maximum_add_fusion.own), channel_id=1, source_target_pairs={{0,3},{1,0},{2,1},{3,2},{4,7},{5,4},{6,5},{7,6},{8,11},{9,8},{10,9... | collective-permute-start | bytes 786440 | tf_op jit(solution)/shard_map/sketch/ppermute | solution.py:36
  45.2 5.1 %collective-permute-start.6 = (f32[64,512]{1,0:T(8,128)S(1)}, f32[64,512]{1,0:T(8,128)S(1)}, u32[]{:S(2)}, u32[]{:S(2)}) collective-permute-start(f32[64,512]{1,0:T(8,128)S(1)} %slice.22), channel_id=1, source_target_pairs={{0,1},{1,2},{2,3},{3,0},{4,5},{5,6},{6,7},{7,4},{8,9},{9,10},{10,1... | collective-permute-start | bytes 393224 | tf_op jit(solution)/shard_map/sketch/ppermute | solution.py:36
  45.5 4.8 %collective-permute-start.7 = (f32[64,512]{1,0:T(8,128)S(1)}, f32[64,512]{1,0:T(8,128)S(1)}, u32[]{:S(2)}, u32[]{:S(2)}) collective-permute-start(f32[64,512]{1,0:T(8,128)S(1)} %slice.23), channel_id=1, source_target_pairs={{0,3},{1,0},{2,1},{3,2},{4,7},{5,4},{6,5},{7,6},{8,11},{9,8},{10,9... | collective-permute-start | bytes 393224 | tf_op jit(solution)/shard_map/sketch/ppermute | solution.py:36
  50.4 5.9 %copy-start = (f32[4,128,512]{2,1,0:T(8,128)}, f32[4,128,512]{2,1,0:T(8,128)S(1)}, u32[]{:S(2)}) copy-start(f32[4,128,512]{2,1,0:T(8,128)S(1)} %place_blocks.1) | copy-start | bytes 3145732
  50.4 5.9 %collective-permute-start.8 = (f32[512,512]{1,0:T(8,128)S(1)}, f32[512,512]{1,0:T(8,128)S(1)}, u32[]{:S(2)}, u32[]{:S(2)}) collective-permute-start(f32[512,512]{1,0:T(8,128)S(1)} %bitcast.20), channel_id=1, source_target_pairs={{0,4},{4,0},{8,12},{12,8},{16,20},{20,16},{24,28},{28,24},{32,36},... | collective-permute-start | bytes 3145736 | tf_op jit(solution)/shard_map/sketch/ppermute | solution.py:40
  56.3 1.0 copy-start.2
  114.4 6.4 %collective-permute-start.10 = (f32[4,64,512]{2,1,0:T(8,128)S(1)}, f32[4,64,512]{2,1,0:T(8,128)S(1)}, u32[]{:S(2)}, u32[]{:S(2)}) collective-permute-start(f32[4,64,512]{2,1,0:T(8,128)S(1)} %all_to_all.22), channel_id=1, source_target_pairs={{0,4},{4,0},{8,12},{12,8},{16,20},{20,16},{24,28},{28,24},{32,36},... | collective-permute-start | bytes 1572872 | tf_op jit(solution)/shard_map/gram/ppermute | solution.py:40
  133.6 1.0 copy-start.1
  140.9 22.3 %all-to-all-start.3 = ((f32[64,8,256]{2,1,0:T(8,128)}), f32[64,8,256]{2,1,0:T(8,128)S(1)}, u32[]{:S(2)}, u32[]{:S(2)}) async-start(f32[64,8,256]{2,1,0:T(8,128)} %bitcast.9), calls=%async_computation.4 | async-start | bytes 1048576 | tf_op jit(solution)/shard_map/apply/all_to_all | solution.py:44
Sparse Core Ops, SparseCore 0:
  69.6 60.0 reduce-scatter.1

commit v5 on v3

--- a/solution.py
+++ b/solution.py
@@ -370,13 +370,16 @@
     )(gram, *upper, *inverse)
 
 
-def factorize(gram):
+def factorize(gram, total):
     upper, inverse = [], []
-    for d in range(gram.shape[0] // BLOCK):
+    last = gram.shape[0] // BLOCK - 1
+    for d in range(last + 1):
+        if d == last:
+            gram, total = together(gram, total)
         up, inv = factor_step(d, gram, upper, inverse)
         upper.append(up)
         inverse.append(inv)
-    return jnp.concatenate(upper, 0), inverse
+    return jnp.concatenate(upper, 0), inverse, total
 
 
 def apply_kernel(scale, total_ref, *refs):
@@ -454,7 +457,7 @@
         gram = gram.transpose(1, 0, 2, 3).reshape(rank, rank)
 
     with jax.named_scope("factor"):
-        upper, inverse = factorize(gram)
+        upper, inverse, total = factorize(gram, total)
 
     with jax.named_scope("apply"):
         result = apply_inverse(inverse, total, norm_scale)

time: 171 us -> 170 us (level)
  transfers between devices with their start and end apart: 13 -> 13, of which waited for: 6 -> 6; matrix products, arithmetic and copies ran while one was open for 2% -> 2% of each run, Pallas kernels for 20% -> 17%
where the time goes in v5:
time: 170 us
  Pallas kernels  47.6 us (28%)
  blocking collectives  44.6 us (26%)
  waiting for transfers between devices  31 us (18%)
  starting transfers between devices  27.3 us (16%)
  between operations  14.3 us (8%)
  other arithmetic  2.77 us (2%)
  local copies, waits for them, and re-layouts  2.19 us (1%)
    all_to_all x2, blocking collectives, exchange(): return lax.all_to_all(array, 'row', 0, 0, axis_index_groups=groups)  33.6 us
    pallas_call x4, Pallas kernels, factor_step(): pl.pallas_call(functools.partial(factor_kernel, d), in_specs=[IN_VMEM] *...  17.3 us
    all_to_all x1, waiting for transfers between devices, exchange(): return lax.all_to_all(array, 'row', 0, 0, axis_index_groups=groups)  17.2 us
    pallas_call x2, Pallas kernels, sketch_product(): pl.pallas_call(functools.partial(sketch_kernel, pieces), in_specs=[IN_SME...  16.4 us
    pallas_call x1, Pallas kernels, chip_products(): pl.pallas_call(chip_kernel, in_specs=[IN_SMEM] * 2 + [IN_VMEM] * 2 + [IN_...  12.2 us
    ppermute x3, starting transfers between devices, swap_core(): return lax.ppermute(array, 'row', row_pairs(lambda z, x, c: (z, x, 1 - c)))  11.8 us
    ppermute x8, starting transfers between devices, send_y(): return lax.ppermute(array, 'col', [(i, (i + step) % YS) for i in range(YS)])  11.1 us
    all_to_all x1, blocking collectives, shards(): gram = lax.all_to_all(repeat(gram, YS), 'col', 0, 0)  11 us
  transfers between devices with their start and end apart: 13, of which 6 were waited for; matrix products, arithmetic and copies ran while one was open for 2% of the time, Pallas kernels for 17%

profile of v5, /device:TPU:1, one launch (start us, length us, event | category | flops | bytes accessed | tf_op | source)
XLA Modules:
  0.0 169.7 jit_solution(9439932473741007019)
XLA Ops:
  7.2 3.3 %collective-permute-start.9 = (f32[512,4096]{1,0:T(8,128)}, f32[512,4096]{1,0:T(8,128)}, u32[]{:S(2)}, u32[]{:S(2)}) collective-permute-start(f32[512,4096]{1,0:T(8,128)} %panel_ref.3), channel_id=1, source_target_pairs={{0,4},{4,0},{8,12},{12,8},{16,20},{20,16},{24,28},{28,24},{32,36},... | collective-permute-start | bytes 25165832 | tf_op jit(solution)/shard_map/sketch/ppermute | solution.py:40
  10.5 8.4 %sketch_product.2 = (f32[128,512]{1,0:T(8,128)}, f32[128,512]{1,0:T(8,128)}) custom-call(s32[1]{0:T(128)} %bitcast.y_ref, f32[512,4096]{1,0:T(8,128)} %panel_ref.3, f32[4096,512]{1,0:T(8,128)} %matrix_ref.3), custom_call_target="tpu_custom_call" | custom-call | flops 3221225472 | bytes 12582912 | tf_op jit(solution)/shard_map/sketch/sketch_product/pallas_call | solution.py:148
  19.0 2.7 %collective-permute-start.1 = (f32[128,512]{1,0:T(8,128)}, f32[128,512]{1,0:T(8,128)S(1)}, u32[]{:S(2)}, u32[]{:S(2)}) collective-permute-start(f32[128,512]{1,0:T(8,128)} %get-tuple-element.35), channel_id=1, source_target_pairs={{0,3},{1,0},{2,1},{3,2},{4,7},{5,4},{6,5},{7,6},{8,11},{9,8},{10,9... | collective-permute-start | bytes 786440 | tf_op jit(solution)/shard_map/sketch/ppermute | solution.py:36
  21.7 8.1 %sketch_product.3 = (f32[64,512]{1,0:T(8,128)}, f32[64,512]{1,0:T(8,128)}, f32[128,512]{1,0:T(8,128)}) custom-call(s32[1]{0:T(128)} %bitcast.y_ref, f32[512,4096]{1,0:T(8,128)} %panel_ref.3, f32[4096,512]{1,0:T(8,128)} %matrix_ref.3), custom_call_target="tpu_custom_call" | custom-call | flops 3221225472 | bytes 12582912 | tf_op jit(solution)/shard_map/sketch/sketch_product/pallas_call | solution.py:148
  30.9 2.7 %collective-permute-start.3 = (f32[64,512]{1,0:T(8,128)S(1)}, f32[64,512]{1,0:T(8,128)S(1)}, u32[]{:S(2)}, u32[]{:S(2)}) collective-permute-start(f32[64,512]{1,0:T(8,128)S(1)} %get-tuple-element.41), channel_id=1, source_target_pairs={{0,3},{1,0},{2,1},{3,2},{4,7},{5,4},{6,5},{7,6},{8,11},{9,8},{10,9... | collective-permute-start | bytes 393224 | tf_op jit(solution)/shard_map/sketch/ppermute | solution.py:36
  33.5 3.0 %collective-permute-done.2 = f32[64,512]{1,0:T(8,128)S(1)} collective-permute-done((f32[64,512]{1,0:T(8,128)S(1)}, f32[64,512]{1,0:T(8,128)S(1)}, u32[]{:S(2)}, u32[]{:S(2)}) %collective-permute-start.2) | collective-permute-done | bytes 131104 | tf_op jit(solution)/shard_map/sketch/ppermute | solution.py:36
  37.7 2.7 %collective-permute-start.5 = (f32[128,512]{1,0:T(8,128)S(1)}, f32[128,512]{1,0:T(8,128)S(1)}, u32[]{:S(2)}, u32[]{:S(2)}) collective-permute-start(f32[128,512]{1,0:T(8,128)S(1)} %maximum_add_fusion.own), channel_id=1, source_target_pairs={{0,3},{1,0},{2,1},{3,2},{4,7},{5,4},{6,5},{7,6},{8,11},{9,8},{10,9... | collective-permute-start | bytes 786440 | tf_op jit(solution)/shard_map/sketch/ppermute | solution.py:36
  40.3 4.9 %collective-permute-done.4.before = f32[128,512]{1,0:T(8,128)S(1)} collective-permute-done((f32[128,512]{1,0:T(8,128)S(1)}, f32[128,512]{1,0:T(8,128)S(1)}, u32[]{:S(2)}, u32[]{:S(2)}) %collective-permute-start.4) | collective-permute-done | bytes 262176 | tf_op jit(solution)/shard_map/sketch/ppermute | solution.py:36
  45.5 2.5 %collective-permute-start.7 = (f32[64,512]{1,0:T(8,128)S(1)}, f32[64,512]{1,0:T(8,128)S(1)}, u32[]{:S(2)}, u32[]{:S(2)}) collective-permute-start(f32[64,512]{1,0:T(8,128)S(1)} %slice.23), channel_id=1, source_target_pairs={{0,3},{1,0},{2,1},{3,2},{4,7},{5,4},{6,5},{7,6},{8,11},{9,8},{10,9... | collective-permute-start | bytes 393224 | tf_op jit(solution)/shard_map/sketch/ppermute | solution.py:36
  48.1 2.3 %collective-permute-done.6.head = f32[64,512]{1,0:T(8,128)S(1)} collective-permute-done((f32[64,512]{1,0:T(8,128)S(1)}, f32[64,512]{1,0:T(8,128)S(1)}, u32[]{:S(2)}, u32[]{:S(2)}) %collective-permute-start.6) | collective-permute-done | bytes 131104 | tf_op jit(solution)/shard_map/sketch/ppermute | solution.py:36
  50.4 3.6 %collective-permute-start.8 = (f32[512,512]{1,0:T(8,128)S(1)}, f32[512,512]{1,0:T(8,128)S(1)}, u32[]{:S(2)}, u32[]{:S(2)}) collective-permute-start(f32[512,512]{1,0:T(8,128)S(1)} %bitcast.20), channel_id=1, source_target_pairs={{0,4},{4,0},{8,12},{12,8},{16,20},{20,16},{24,28},{28,24},{32,36},... | collective-permute-start | bytes 3145736 | tf_op jit(solution)/shard_map/sketch/ppermute | solution.py:40
  54.0 2.3 %collective-permute-done.8.other_ref = f32[512,512]{1,0:T(8,128)S(1)} collective-permute-done((f32[512,512]{1,0:T(8,128)S(1)}, f32[512,512]{1,0:T(8,128)S(1)}, u32[]{:S(2)}, u32[]{:S(2)}) %collective-permute-start.8) | collective-permute-done | bytes 1048608 | tf_op jit(solution)/shard_map/sketch/ppermute | solution.py:40
  57.3 12.2 %chip_products.1 = (f32[32,2,512]{2,1,0:T(2,128)}, f32[2048,512]{1,0:T(8,128)}) custom-call(s32[1]{0:T(128)} %bitcast.y_ref, s32[1]{0:T(128)} %bitcast.1.core_ref, f32[512,512]{1,0:T(8,128)} %bitcast.21, f32[512,512]{1,0:T(8,128)} %copy-done.2, f32[512,4096]{1,0:T(8,128)} %panel_ref.3, f32[512,4096]{1,0:T(8,128)} %collective-permute-done.9.arrived_ref), custom_call_target="tpu_custom_call" | custom-call | flops 6442450944 | bytes 25165824 | tf_op jit(solution)/shard_map/project/chip_products/pallas_call | solution.py:247
  69.5 19.0 %all_to_all.20 = f32[32,2,512]{2,1,0:T(2,128)S(1)} all-to-all(f32[32,2,512]{2,1,0:T(2,128)} %get-tuple-element.46), channel_id=1, replica_groups={{0,8,16,24,32,40,48,56,64,72,80,88,96,104,112,120,128,136,144,152,160,1..., dimensions={0} | all-to-all | bytes 262144 | tf_op jit(solution)/shard_map/gram/all_to_all | solution.py:44
  88.6 14.6 %all_to_all.21 = f32[32,2,512]{2,1,0:T(2,128)S(1)} all-to-all(f32[32,2,512]{2,1,0:T(2,128)S(1)} %broadcast_in_dim.24), channel_id=1, replica_groups={{0,8,16,24,32,40,48,56,64,72,80,88,96,104,112,120,128,136,144,152,160,1..., dimensions={0} | all-to-all | bytes 262144 | tf_op jit(solution)/shard_map/gram/all_to_all | solution.py:44
  103.4 11.0 %all_to_all.22 = f32[4,64,512]{2,1,0:T(8,128)S(1)} all-to-all(f32[4,64,512]{2,1,0:T(8,128)S(1)} %broadcast_in_dim.26), channel_id=1, replica_groups=mesh['row'=64,'col'=4] {'col'}, dimensions={0} | all-to-all | bytes 1048576 | tf_op jit(solution)/shard_map/gram/all_to_all | solution.py:455
  114.4 4.8 %collective-permute-start.10 = (f32[4,64,512]{2,1,0:T(8,128)S(1)}, f32[4,64,512]{2,1,0:T(8,128)S(1)}, u32[]{:S(2)}, u32[]{:S(2)}) collective-permute-start(f32[4,64,512]{2,1,0:T(8,128)S(1)} %all_to_all.22), channel_id=1, source_target_pairs={{0,4},{4,0},{8,12},{12,8},{16,20},{20,16},{24,28},{28,24},{32,36},... | collective-permute-start | bytes 1572872 | tf_op jit(solution)/shard_map/gram/ppermute | solution.py:40
  120.8 4.1 %factor_step.4 = (f32[128,512]{1,0:T(8,128)S(1)}, f32[128,512]{1,0:T(8,128)S(1)}) custom-call(f32[512,512]{1,0:T(8,128)S(1)} %bitcast.22), custom_call_target="tpu_custom_call" | custom-call | flops 5000000000 | bytes 786432 | tf_op jit(solution)/shard_map/factor/factor_step/pallas_call | solution.py:361
  124.8 4.3 %factor_step.5 = (f32[128,512]{1,0:T(8,128)S(1)}, f32[128,512]{1,0:T(8,128)S(1)}) custom-call(f32[512,512]{1,0:T(8,128)S(1)} %bitcast.23, f32[128,512]{1,0:T(8,128)S(1)} %get-tuple-element.50.refs_1_, f32[128,512]{1,0:T(8,128)S(1)} %get-tuple-element.49.refs_2_.refs_3_.refs_4_.refs_0_), custom_call_target="tpu_custom_call" | custom-call | flops 5000000000 | bytes 1310720 | tf_op jit(solution)/shard_map/factor/factor_step/pallas_call | solution.py:361
  129.2 4.4 %factor_step.6 = (f32[128,512]{1,0:T(8,128)S(1)}, f32[128,512]{1,0:T(8,128)S(1)}) custom-call(f32[512,512]{1,0:T(8,128)S(1)} %bitcast.24, f32[128,512]{1,0:T(8,128)S(1)} %get-tuple-element.50.refs_1_, f32[128,512]{1,0:T(8,128)S(1)} %get-tuple-element.52.refs_2_, f32[128,512]{1,0:T(8,128)S(1)} %get-tuple-element.49.refs_2_.refs_3_.refs_4_.refs_0_, ...), custom_call_target="tpu_custom_call" | custom-call | flops 5000000000 | bytes 1835008 | tf_op jit(solution)/shard_map/factor/factor_step/pallas_call | solution.py:361
  133.7 4.5 %factor_step.7 = (f32[128,512]{1,0:T(8,128)S(1)}, f32[128,512]{1,0:T(8,128)S(1)}) custom-call(f32[512,512]{1,0:T(8,128)S(1)} %bitcast.25, f32[128,512]{1,0:T(8,128)S(1)} %get-tuple-element.50.refs_1_, f32[128,512]{1,0:T(8,128)S(1)} %get-tuple-element.52.refs_2_, f32[128,512]{1,0:T(8,128)S(1)} %get-tuple-element.55.refs_3_, ...), custom_call_target="tpu_custom_call" | custom-call | flops 5000000000 | bytes 2359296 | tf_op jit(solution)/shard_map/factor/factor_step/pallas_call | solution.py:361
  138.1 1.6 apply_inverse.1
  139.7 4.5 %all-to-all-start.3 = ((f32[64,8,256]{2,1,0:T(8,128)}), f32[64,8,256]{2,1,0:T(8,128)S(1)}, u32[]{:S(2)}, u32[]{:S(2)}) async-start(f32[64,8,256]{2,1,0:T(8,128)} %bitcast.9), calls=%async_computation.4 | async-start | bytes 1048576 | tf_op jit(solution)/shard_map/apply/all_to_all | solution.py:44
  144.8 17.2 %all-to-all-done.3 = f32[64,8,256]{2,1,0:T(8,128)S(1)} async-done(((f32[64,8,256]{2,1,0:T(8,128)}), f32[64,8,256]{2,1,0:T(8,128)S(1)}, u32[]{:S(2)}, u32[]{:S(2)}) %all-to-all-start.3) | async-done | bytes 524320 | tf_op jit(solution)/shard_map/apply/all_to_all | solution.py:44
  (38 shorter events, 7.0 us)
Async XLA Ops:
  7.2 126.5 %reduce-scatter.2.cloned.1.call-start = ((), (), s32[]{:S(2)}) async-start(), calls=%async_computation.5 | async-start | bytes 4718592 | tf_op jit(solution)/shard_map/project/reduce_scatter | solution.py:448
  7.2 49.1 %collective-permute-start.9 = (f32[512,4096]{1,0:T(8,128)}, f32[512,4096]{1,0:T(8,128)}, u32[]{:S(2)}, u32[]{:S(2)}) collective-permute-start(f32[512,4096]{1,0:T(8,128)} %panel_ref.3), channel_id=1, source_target_pairs={{0,4},{4,0},{8,12},{12,8},{16,20},{20,16},{24,28},{28,24},{32,36},... | collective-permute-start | bytes 25165832 | tf_op jit(solution)/shard_map/sketch/ppermute | solution.py:40
  18.9 10.8 %collective-permute-start = (f32[128,512]{1,0:T(8,128)}, f32[128,512]{1,0:T(8,128)S(1)}, u32[]{:S(2)}, u32[]{:S(2)}) collective-permute-start(f32[128,512]{1,0:T(8,128)} %get-tuple-element.34), channel_id=1, source_target_pairs={{0,1},{1,2},{2,3},{3,0},{4,5},{5,6},{6,7},{7,4},{8,9},{9,10},{10,1... | collective-permute-start | bytes 786440 | tf_op jit(solution)/shard_map/sketch/ppermute | solution.py:36
  19.0 10.8 %collective-permute-start.1 = (f32[128,512]{1,0:T(8,128)}, f32[128,512]{1,0:T(8,128)S(1)}, u32[]{:S(2)}, u32[]{:S(2)}) collective-permute-start(f32[128,512]{1,0:T(8,128)} %get-tuple-element.35), channel_id=1, source_target_pairs={{0,3},{1,0},{2,1},{3,2},{4,7},{5,4},{6,5},{7,6},{8,11},{9,8},{10,9... | collective-permute-start | bytes 786440 | tf_op jit(solution)/shard_map/sketch/ppermute | solution.py:36
  30.8 5.7 %collective-permute-start.2 = (f32[64,512]{1,0:T(8,128)S(1)}, f32[64,512]{1,0:T(8,128)S(1)}, u32[]{:S(2)}, u32[]{:S(2)}) collective-permute-start(f32[64,512]{1,0:T(8,128)S(1)} %get-tuple-element.40), channel_id=1, source_target_pairs={{0,1},{1,2},{2,3},{3,0},{4,5},{5,6},{6,7},{7,4},{8,9},{9,10},{10,1... | collective-permute-start | bytes 393224 | tf_op jit(solution)/shard_map/sketch/ppermute | solution.py:36
  30.9 5.7 %collective-permute-start.3 = (f32[64,512]{1,0:T(8,128)S(1)}, f32[64,512]{1,0:T(8,128)S(1)}, u32[]{:S(2)}, u32[]{:S(2)}) collective-permute-start(f32[64,512]{1,0:T(8,128)S(1)} %get-tuple-element.41), channel_id=1, source_target_pairs={{0,3},{1,0},{2,1},{3,2},{4,7},{5,4},{6,5},{7,6},{8,11},{9,8},{10,9... | collective-permute-start | bytes 393224 | tf_op jit(solution)/shard_map/sketch/ppermute | solution.py:36
  37.6 7.6 %collective-permute-start.4 = (f32[128,512]{1,0:T(8,128)S(1)}, f32[128,512]{1,0:T(8,128)S(1)}, u32[]{:S(2)}, u32[]{:S(2)}) collective-permute-start(f32[128,512]{1,0:T(8,128)S(1)} %maximum_add_fusion.own), channel_id=1, source_target_pairs={{0,1},{1,2},{2,3},{3,0},{4,5},{5,6},{6,7},{7,4},{8,9},{9,10},{10,1... | collective-permute-start | bytes 786440 | tf_op jit(solution)/shard_map/sketch/ppermute | solution.py:36
  37.7 7.5 %collective-permute-start.5 = (f32[128,512]{1,0:T(8,128)S(1)}, f32[128,512]{1,0:T(8,128)S(1)}, u32[]{:S(2)}, u32[]{:S(2)}) collective-permute-start(f32[128,512]{1,0:T(8,128)S(1)} %maximum_add_fusion.own), channel_id=1, source_target_pairs={{0,3},{1,0},{2,1},{3,2},{4,7},{5,4},{6,5},{7,6},{8,11},{9,8},{10,9... | collective-permute-start | bytes 786440 | tf_op jit(solution)/shard_map/sketch/ppermute | solution.py:36
  45.2 5.1 %collective-permute-start.6 = (f32[64,512]{1,0:T(8,128)S(1)}, f32[64,512]{1,0:T(8,128)S(1)}, u32[]{:S(2)}, u32[]{:S(2)}) collective-permute-start(f32[64,512]{1,0:T(8,128)S(1)} %slice.22), channel_id=1, source_target_pairs={{0,1},{1,2},{2,3},{3,0},{4,5},{5,6},{6,7},{7,4},{8,9},{9,10},{10,1... | collective-permute-start | bytes 393224 | tf_op jit(solution)/shard_map/sketch/ppermute | solution.py:36
  45.5 4.8 %collective-permute-start.7 = (f32[64,512]{1,0:T(8,128)S(1)}, f32[64,512]{1,0:T(8,128)S(1)}, u32[]{:S(2)}, u32[]{:S(2)}) collective-permute-start(f32[64,512]{1,0:T(8,128)S(1)} %slice.23), channel_id=1, source_target_pairs={{0,3},{1,0},{2,1},{3,2},{4,7},{5,4},{6,5},{7,6},{8,11},{9,8},{10,9... | collective-permute-start | bytes 393224 | tf_op jit(solution)/shard_map/sketch/ppermute | solution.py:36
  50.4 5.9 %copy-start = (f32[4,128,512]{2,1,0:T(8,128)}, f32[4,128,512]{2,1,0:T(8,128)S(1)}, u32[]{:S(2)}) copy-start(f32[4,128,512]{2,1,0:T(8,128)S(1)} %place_blocks.1) | copy-start | bytes 3145732
  50.4 5.9 %collective-permute-start.8 = (f32[512,512]{1,0:T(8,128)S(1)}, f32[512,512]{1,0:T(8,128)S(1)}, u32[]{:S(2)}, u32[]{:S(2)}) collective-permute-start(f32[512,512]{1,0:T(8,128)S(1)} %bitcast.20), channel_id=1, source_target_pairs={{0,4},{4,0},{8,12},{12,8},{16,20},{20,16},{24,28},{28,24},{32,36},... | collective-permute-start | bytes 3145736 | tf_op jit(solution)/shard_map/sketch/ppermute | solution.py:40
  56.3 1.0 copy-start.2
  114.4 6.4 %collective-permute-start.10 = (f32[4,64,512]{2,1,0:T(8,128)S(1)}, f32[4,64,512]{2,1,0:T(8,128)S(1)}, u32[]{:S(2)}, u32[]{:S(2)}) collective-permute-start(f32[4,64,512]{2,1,0:T(8,128)S(1)} %all_to_all.22), channel_id=1, source_target_pairs={{0,4},{4,0},{8,12},{12,8},{16,20},{20,16},{24,28},{28,24},{32,36},... | collective-permute-start | bytes 1572872 | tf_op jit(solution)/shard_map/gram/ppermute | solution.py:40
  133.6 4.5 %copy-start.1 = (f32[256,512]{1,0:T(8,128)S(1)}, f32[256,512]{1,0:T(8,128)}, u32[]{:S(2)}) copy-start(f32[256,512]{1,0:T(8,128)} %reduce-scatter.2.cloned.1.call-done.total_ref) | copy-start | bytes 1572868
  139.7 22.3 %all-to-all-start.3 = ((f32[64,8,256]{2,1,0:T(8,128)}), f32[64,8,256]{2,1,0:T(8,128)S(1)}, u32[]{:S(2)}, u32[]{:S(2)}) async-start(f32[64,8,256]{2,1,0:T(8,128)} %bitcast.9), calls=%async_computation.4 | async-start | bytes 1048576 | tf_op jit(solution)/shard_map/apply/all_to_all | solution.py:44
Sparse Core Ops, SparseCore 0:
  69.6 60.0 reduce-scatter.1
